TPU v7x, 32 devices: a whole 2x2x4 slice. The times are simulated.
32 devices in a mesh: rep: 2 (over y), fsdp: 16 (over z, x, core).
Axes of the slice: x: 2, y: 2, z: 4, core: 2. Of those that a mesh axis runs over, the one named last changes fastest.
Arguments:
- tracker: bfloat16 [2, 16, 128, 5120], P('rep', None, 'fsdp'), may hold values from -40 to 40
- levels: bfloat16 [2, 16, 128, 5120], P('rep', None, 'fsdp'), may hold values from -127 to 127, as said below
- exponents: int32 [2, 16, 128], P('rep', None, 'fsdp'), may hold values from -8 to -5
Outputs:
- update: bfloat16 [2, 16, 128, 5120], P('rep', None, 'fsdp')
Inputs may be any that keep to these rules, and one draw needn't show every extreme that they name: `levels`: whole numbers.
All inputs are finite; a program needn't handle non-finite values.
Results may differ from a plain program's by a relative error of at most 0.025.
Values may be sent and summed in bfloat16 or wider, within the bound.
No kernel may reach another device: no remote copies, remote signals or barrier semaphores. Data moves between devices by JAX's collectives and lax.ppermute only.
A program may use at most 64 MiB of HBM per device.

v0:
```python
import math

import jax
import jax.numpy as jnp
from jax import lax
from jax.sharding import PartitionSpec as P

NS_STEPS = 5


gamma_mix = 0.5
coef_a = 3.4445
coef_b = -4.775
coef_c = 2.0315


def shifted(block, axis, distance):
    devices = range(lax.axis_size(axis))
    route = [((i - distance) % len(devices), i) for i in devices]
    return lax.ppermute(block, axis, route)


def orthogonalize(matrix, columns):
    values = matrix.astype(jnp.float32)
    frobenius = jnp.sqrt(jnp.sum(values * values))
    iterate = (values / (frobenius + 1e-07)).astype(jnp.bfloat16)
    for iteration in range(NS_STEPS):
        gram_mat = lax.dot_general(
            iterate, iterate, (((1,), (1,)), ((), ())), preferred_element_type=jnp.float32
        ).astype(jnp.bfloat16)
        square = jnp.dot(gram_mat, gram_mat, preferred_element_type=jnp.float32)
        polynomial = (coef_b * gram_mat.astype(jnp.float32) + coef_c * square).astype(jnp.bfloat16)
        iterate = (
            coef_a * iterate.astype(jnp.float32)
            + jnp.dot(polynomial, iterate, preferred_element_type=jnp.float32)
        ).astype(jnp.bfloat16)
    factor = 2.0 ** (int(math.log2(columns)) // 2)
    return (iterate.astype(jnp.float32) * factor).astype(jnp.bfloat16)


def per_device(tracker, levels, exponents):
    powers = jnp.exp2(exponents.astype(jnp.float32))[..., None]
    message = (levels.astype(jnp.float32) * powers).astype(jnp.bfloat16)
    from_left = shifted(message, "rep", 1)
    from_right = shifted(message, "rep", -1)
    mixed_rows = (
        tracker.astype(jnp.float32)
        + gamma_mix
        * (
            from_left.astype(jnp.float32)
            + from_right.astype(jnp.float32)
            - 2.0 * message.astype(jnp.float32)
        )
    ).astype(jnp.bfloat16)
    columns = tracker.shape[3]
    owned_rows = lax.all_to_all(mixed_rows, "fsdp", split_axis=1, concat_axis=2, tiled=True)
    result = orthogonalize(owned_rows[0, 0], columns)[None, None]
    return lax.all_to_all(result, "fsdp", split_axis=2, concat_axis=1, tiled=True)


def solution(mesh):
    in_specs = (P("rep", None, "fsdp", None), P("rep", None, "fsdp", None), P("rep", None, "fsdp"))
    out_specs = P("rep", None, "fsdp", None)
    return jax.shard_map(
        per_device, mesh=mesh, in_specs=in_specs, out_specs=out_specs, check_vma=False
    )
```

profile of v0, /device:TPU:1, one launch (start us, length us, event | category | flops | bytes accessed | tf_op | source)
XLA Modules:
  0.0 141.0 jit_solution(16569702023717137440)
XLA Ops:
  0.0 0.7 exponential_bitcast_fusion
  0.7 0.1 copy.11
  0.8 0.0 copy-start
  0.8 0.0 copy-start.1
  0.8 1.8 %multiply_convert_fusion = bf16[1,16,8,5120]{3,2,0,1:T(8,128)(2,1)S(1)} fusion(bf16[1,16,8,5120]{3,2,1,0:T(8,128)(2,1)} %param.4, f32[16,8]{1,0:T(8,128)S(1)} %copy.11), kind=kLoop, calls=%fused_computation.19 | loop fusion | flops 1966080 | bytes 2621952 | tf_op jit(solution)/shard_map/convert_element_type | solution.py:43
  2.5 2.1 %collective-permute-start = (bf16[1,16,8,5120]{3,2,0,1:T(8,128)(2,1)S(1)}, bf16[1,16,8,5120]{3,2,0,1:T(8,128)(2,1)S(1)}, u32[]{:S(2)}, u32[]{:S(2)}) collective-permute-start(bf16[1,16,8,5120]{3,2,0,1:T(8,128)(2,1)S(1)} %multiply_convert_fusion), channel_id=1, source_target_pairs={{16,0},{0,16},{17,1},{1,17},{18,2},{2,18},{19,3},{3,19},{20,4},{4,... | collective-permute-start | bytes 3932168 | tf_op jit(solution)/shard_map/ppermute | solution.py:20
  4.7 28.5 %collective-permute-done = bf16[1,16,8,5120]{3,2,0,1:T(8,128)(2,1)S(1)} collective-permute-done((bf16[1,16,8,5120]{3,2,0,1:T(8,128)(2,1)S(1)}, bf16[1,16,8,5120]{3,2,0,1:T(8,128)(2,1)S(1)}, u32[]{:S(2)}, u32[]{:S(2)}) %collective-permute-start) | collective-permute-done | bytes 1310752 | tf_op jit(solution)/shard_map/ppermute | solution.py:20
  33.2 0.0 copy-done
  33.2 0.0 copy-done.1
  33.2 0.9 add_convert_fusion
  34.1 38.9 %all_to_all.21 = bf16[1,16,8,5120]{3,2,0,1:T(8,128)(2,1)S(1)} all-to-all(bf16[1,16,8,5120]{3,2,0,1:T(8,128)(2,1)S(1)} %add_convert_fusion), channel_id=1, replica_groups=mesh['rep'=2,'fsdp'=16] {'fsdp'}, dimensions={1} | all-to-all | bytes 2621440 | tf_op jit(solution)/shard_map/all_to_all | solution.py:56
  73.0 1.3 fusion.9
  75.0 0.6 convolution_convert_fusion.4
  75.5 0.8 fusion
  76.4 0.5 convolution_convert_fusion.3
  76.9 0.6 fusion.1
  77.5 0.5 convolution_convert_fusion.2
  78.0 0.6 fusion.2
  78.7 0.5 convolution_convert_fusion.1
  79.2 0.6 fusion.3
  79.8 0.5 convolution_convert_fusion
  80.3 1.8 %fusion.8 = bf16[1,1,128,5120]{3,2,1,0:T(8,128)(2,1)} fusion(bf16[128,5120]{1,0:T(8,128)(2,1)S(1)} %fusion.3, bf16[128,128]{1,0:T(8,128)(2,1)S(1)} %convolution_convert_fusion), kind=kOutput, calls=%fused_computation.13 | convolution fusion | flops 176635904 | bytes 2654208 | tf_op jit(solution)/shard_map/dot_general | solution.py:35
  82.2 3.3 %copy.17 = bf16[1,1,128,5120]{3,1,0,2:T(2,128)(2,1)S(1)} copy(bf16[1,1,128,5120]{3,2,1,0:T(8,128)(2,1)} %fusion.8) | data formatting | bytes 2621440 | tf_op jit(solution)/shard_map/broadcast_in_dim | solution.py:57
  85.5 0.6 broadcast.67
  86.1 9.8 %reduce.2 = bf16[128,5120]{1,0:T(8,128)(2,1)} reduce(bf16[128,1,1,5120]{3,2,1,0:T(2,128)(2,1)S(1)} %bitcast.46, bf16[]{:T(256)} %broadcast.67), dimensions={1,2}, to_apply=%bitcast.45.reduce_sub_computation | reduce | bytes 2621442
  96.0 3.6 %reshape.26 = bf16[16,2,20480]{2,1,0:T(2,128)(2,1)S(1)} reshape(bf16[128,5120]{1,0:T(8,128)(2,1)} %reduce.2) | data formatting | bytes 2621440
  99.6 35.4 %all_to_all.22 = bf16[16,2,20480]{2,1,0:T(2,128)(2,1)} all-to-all(bf16[16,2,20480]{2,1,0:T(2,128)(2,1)S(1)} %reshape.26), channel_id=1, replica_groups=mesh['rep'=2,'fsdp'=16] {'fsdp'}, dimensions={0} | all-to-all | bytes 2621440 | tf_op jit(solution)/shard_map/all_to_all | solution.py:58
  135.0 4.5 %reshape.27 = bf16[128,1,1,5120]{3,2,1,0:T(2,128)(2,1)S(1)} reshape(bf16[16,2,20480]{2,1,0:T(2,128)(2,1)} %all_to_all.22) | data formatting | bytes 2621440
  139.5 1.5 %copy.16 = bf16[1,1,128,5120]{3,2,0,1:T(8,128)(2,1)} copy(bf16[1,1,128,5120]{3,1,0,2:T(2,128)(2,1)S(1)} %bitcast.47) | data formatting | bytes 2621440
Async XLA Ops:
  0.8 32.4 %copy-start = (bf16[1,16,8,5120]{3,2,1,0:T(8,128)(2,1)S(1)}, bf16[1,16,8,5120]{3,2,1,0:T(8,128)(2,1)}, u32[]{:S(2)}) copy-start(bf16[1,16,8,5120]{3,2,1,0:T(8,128)(2,1)} %param.4) | copy-start | bytes 3932164
  0.8 32.4 %copy-start.1 = (bf16[1,16,8,5120]{3,2,1,0:T(8,128)(2,1)S(1)}, bf16[1,16,8,5120]{3,2,1,0:T(8,128)(2,1)}, u32[]{:S(2)}) copy-start(bf16[1,16,8,5120]{3,2,1,0:T(8,128)(2,1)} %param.3) | copy-start | bytes 3932164
  2.5 30.6 %collective-permute-start = (bf16[1,16,8,5120]{3,2,0,1:T(8,128)(2,1)S(1)}, bf16[1,16,8,5120]{3,2,0,1:T(8,128)(2,1)S(1)}, u32[]{:S(2)}, u32[]{:S(2)}) collective-permute-start(bf16[1,16,8,5120]{3,2,0,1:T(8,128)(2,1)S(1)} %multiply_convert_fusion), channel_id=1, source_target_pairs={{16,0},{0,16},{17,1},{1,17},{18,2},{2,18},{19,3},{3,19},{20,4},{4,... | collective-permute-start | bytes 3932168 | tf_op jit(solution)/shard_map/ppermute | solution.py:20
where the time goes:
time: 141 us
  blocking collectives  74.3 us (53%)
  waiting for transfers between devices  28.5 us (20%)
  other arithmetic  14.4 us (10%)
  local copies, waits for them, and re-layouts  13.6 us (10%)
  matrix products  7.16 us (5%)
  starting transfers between devices  2.13 us (2%)
    all_to_all x1, blocking collectives, per_device(): lax.all_to_all(mixed_rows, 'fsdp', split_axis=1, concat_axis=2, tiled=True)  38.9 us
    all_to_all x1, blocking collectives, per_device(): lax.all_to_all(result, 'fsdp', split_axis=2, concat_axis=1, tiled=True)  35.4 us
    ppermute x1, waiting for transfers between devices, shifted(): return lax.ppermute(block, axis, route)  28.5 us
    unnamed x8, local copies, waits for them, and re-layouts  10.2 us
    unnamed x1, other arithmetic  9.83 us
    dot_general x5, matrix products, orthogonalize(): jnp.dot(polynomial, iterate, preferred_element_type=jnp.float32)  4.58 us
    broadcast_in_dim x1, local copies, waits for them, and re-layouts, per_device(): result = orthogonalize(owned_rows[0, 0], columns)[None, None]  3.34 us
  transfers between devices with their start and end apart: 1, of which 1 were waited for; matrix products, arithmetic and copies ran while one was open for 0% of the time, Pallas kernels for 0%

commit v1 on v0

--- a/solution.py
+++ b/solution.py
@@ -52,10 +52,11 @@
             - 2.0 * message.astype(jnp.float32)
         )
     ).astype(jnp.bfloat16)
-    columns = tracker.shape[3]
-    owned_rows = lax.all_to_all(mixed_rows, "fsdp", split_axis=1, concat_axis=2, tiled=True)
-    result = orthogonalize(owned_rows[0, 0], columns)[None, None]
-    return lax.all_to_all(result, "fsdp", split_axis=2, concat_axis=1, tiled=True)
+    _, mats, rows, columns = tracker.shape
+    owned_rows = lax.all_to_all(mixed_rows[0], "fsdp", split_axis=0, concat_axis=0, tiled=True)
+    result = orthogonalize(owned_rows.reshape(mats * rows, columns), columns)
+    result = result.reshape(mats, rows, columns)
+    return lax.all_to_all(result, "fsdp", split_axis=0, concat_axis=0, tiled=True)[None]
 
 
 def solution(mesh):

time: 141 us -> 118 us (0.84)
  local copies, waits for them, and re-layouts: 13.6 us -> 1.14 us
  other arithmetic: 14.4 us -> 4.6 us
    unnamed x1 -> x0, other arithmetic: 9.83 us -> none
    unnamed x8 -> x5, local copies, waits for them, and re-layouts: 10.2 us -> 1.06 us
    broadcast_in_dim x1 -> x0, local copies, waits for them, and re-layouts: 3.34 us -> none  [per_device(): result = orthogonalize(owned_rows[0, 0], columns)[None, None]]
where the time goes in v1:
time: 118 us; the launch traced here: 117 us
  blocking collectives  74.2 us (63%)
  waiting for transfers between devices  28.5 us (24%)
  matrix products  6.06 us (5%)
  other arithmetic  4.6 us (4%)
  starting transfers between devices  2.13 us (2%)
    all_to_all x1, blocking collectives, per_device(): lax.all_to_all(mixed_rows[0], 'fsdp', split_axis=0, concat_axis=0, tiled=...  38.9 us
    all_to_all x1, blocking collectives, per_device(): lax.all_to_all(result, 'fsdp', split_axis=0, concat_axis=0, tiled=True)  35.3 us
    ppermute x1, waiting for transfers between devices, shifted(): return lax.ppermute(block, axis, route)  28.5 us
    dot_general x5, matrix products, orthogonalize(): jnp.dot(polynomial, iterate, preferred_element_type=jnp.float32)  3.47 us
    dot_general x5, matrix products, orthogonalize(): lax.dot_general(iterate, iterate, (((1,), (1,)), ((), ())), preferred_ele...  2.59 us
  transfers between devices with their start and end apart: 1, of which 1 were waited for; matrix products, arithmetic and copies ran while one was open for 0% of the time, Pallas kernels for 0%

profile of v1, /device:TPU:1, one launch (start us, length us, event | category | flops | bytes accessed | tf_op | source)
XLA Modules:
  0.0 117.4 jit_solution(4800198424055662573)
XLA Ops:
  0.0 0.7 exponential_bitcast_fusion
  0.7 0.1 copy.4
  0.8 0.0 copy-start
  0.8 0.0 copy-start.1
  0.8 1.8 %multiply_convert_fusion = bf16[1,16,8,5120]{3,2,1,0:T(8,128)(2,1)S(1)} fusion(bf16[1,16,8,5120]{3,2,1,0:T(8,128)(2,1)} %param.4, f32[16,8]{1,0:T(8,128)S(1)} %copy.4), kind=kLoop, calls=%fused_computation.19 | loop fusion | flops 1966080 | bytes 2621952 | tf_op jit(solution)/shard_map/convert_element_type | solution.py:43
  2.5 2.1 %collective-permute-start = (bf16[1,16,8,5120]{3,2,1,0:T(8,128)(2,1)S(1)}, bf16[1,16,8,5120]{3,2,1,0:T(8,128)(2,1)S(1)}, u32[]{:S(2)}, u32[]{:S(2)}) collective-permute-start(bf16[1,16,8,5120]{3,2,1,0:T(8,128)(2,1)S(1)} %multiply_convert_fusion), channel_id=1, source_target_pairs={{16,0},{0,16},{17,1},{1,17},{18,2},{2,18},{19,3},{3,19},{20,4},{4,... | collective-permute-start | bytes 3932168 | tf_op jit(solution)/shard_map/ppermute | solution.py:20
  4.7 28.5 %collective-permute-done = bf16[1,16,8,5120]{3,2,1,0:T(8,128)(2,1)S(1)} collective-permute-done((bf16[1,16,8,5120]{3,2,1,0:T(8,128)(2,1)S(1)}, bf16[1,16,8,5120]{3,2,1,0:T(8,128)(2,1)S(1)}, u32[]{:S(2)}, u32[]{:S(2)}) %collective-permute-start) | collective-permute-done | bytes 1310752 | tf_op jit(solution)/shard_map/ppermute | solution.py:20
  33.2 0.0 copy-done
  33.2 0.0 copy-done.1
  33.2 0.9 fusion.11
  34.1 38.9 %all_to_all.10 = bf16[16,8,5120]{2,1,0:T(8,128)(2,1)S(1)} all-to-all(bf16[16,8,5120]{2,1,0:T(8,128)(2,1)S(1)} %fusion.11), channel_id=1, replica_groups=mesh['rep'=2,'fsdp'=16] {'fsdp'}, dimensions={0} | all-to-all | bytes 2621440 | tf_op jit(solution)/shard_map/all_to_all | solution.py:56
  73.0 1.3 %fusion.9 = f32[]{:T(128)} fusion(bf16[16,8,5120]{2,1,0:T(8,128)(2,1)S(1)} %all_to_all.10), kind=kLoop, calls=%fused_computation.16 | loop fusion | flops 1966079 | bytes 1310724 | tf_op jit(solution)/shard_map/reduce_sum | solution.py:25
  75.0 0.6 convolution_convert_fusion.4
  75.5 0.8 fusion
  76.4 0.5 convolution_convert_fusion.3
  76.9 0.6 fusion.1
  77.5 0.5 convolution_convert_fusion.2
  78.0 0.6 fusion.2
  78.7 0.5 convolution_convert_fusion.1
  79.2 0.6 fusion.3
  79.8 0.5 convolution_convert_fusion
  80.3 0.7 fusion.8
  81.1 35.3 %all_to_all.11 = bf16[16,8,5120]{2,1,0:T(8,128)(2,1)S(1)} all-to-all(bf16[16,8,5120]{2,1,0:T(8,128)(2,1)S(1)} %fusion.8), channel_id=1, replica_groups=mesh['rep'=2,'fsdp'=16] {'fsdp'}, dimensions={0} | all-to-all | bytes 2621440 | tf_op jit(solution)/shard_map/all_to_all | solution.py:59
  116.4 1.1 copy.6
Async XLA Ops:
  0.8 32.4 %copy-start = (bf16[1,16,8,5120]{3,2,1,0:T(8,128)(2,1)S(1)}, bf16[1,16,8,5120]{3,2,1,0:T(8,128)(2,1)}, u32[]{:S(2)}) copy-start(bf16[1,16,8,5120]{3,2,1,0:T(8,128)(2,1)} %param.4) | copy-start | bytes 3932164
  0.8 32.4 %copy-start.1 = (bf16[1,16,8,5120]{3,2,1,0:T(8,128)(2,1)S(1)}, bf16[1,16,8,5120]{3,2,1,0:T(8,128)(2,1)}, u32[]{:S(2)}) copy-start(bf16[1,16,8,5120]{3,2,1,0:T(8,128)(2,1)} %param.3) | copy-start | bytes 3932164
  2.5 30.6 %collective-permute-start = (bf16[1,16,8,5120]{3,2,1,0:T(8,128)(2,1)S(1)}, bf16[1,16,8,5120]{3,2,1,0:T(8,128)(2,1)S(1)}, u32[]{:S(2)}, u32[]{:S(2)}) collective-permute-start(bf16[1,16,8,5120]{3,2,1,0:T(8,128)(2,1)S(1)} %multiply_convert_fusion), channel_id=1, source_target_pairs={{16,0},{0,16},{17,1},{1,17},{18,2},{2,18},{19,3},{3,19},{20,4},{4,... | collective-permute-start | bytes 3932168 | tf_op jit(solution)/shard_map/ppermute | solution.py:20

commit v2 on v1

--- a/solution.py
+++ b/solution.py
@@ -1,13 +1,10 @@
 import math
-
 import jax
 import jax.numpy as jnp
 from jax import lax
 from jax.sharding import PartitionSpec as P
 
 NS_STEPS = 5
-
-
 gamma_mix = 0.5
 coef_a = 3.4445
 coef_b = -4.775
@@ -18,6 +15,14 @@
     devices = range(lax.axis_size(axis))
     route = [((i - distance) % len(devices), i) for i in devices]
     return lax.ppermute(block, axis, route)
+
+
+def mix(tracker, message, left, right):
+    f32 = jnp.float32
+    return (
+        tracker.astype(f32)
+        + gamma_mix * (left.astype(f32) + right.astype(f32) - 2.0 * message.astype(f32))
+    ).astype(jnp.bfloat16)
 
 
 def orthogonalize(matrix, columns):
@@ -39,22 +44,43 @@
 
 
 def per_device(tracker, levels, exponents):
+    tracker, levels, exponents = tracker[0], levels[0], exponents[0]
+    mats, rows, columns = tracker.shape
+    half = mats // 2
+    side = lax.axis_index("fsdp") // half
+    halves = [list(range(half)), list(range(half, mats))]
+    far = [(i, (i + half) % mats) for i in range(mats)]
+
     powers = jnp.exp2(exponents.astype(jnp.float32))[..., None]
     message = (levels.astype(jnp.float32) * powers).astype(jnp.bfloat16)
-    from_left = shifted(message, "rep", 1)
-    from_right = shifted(message, "rep", -1)
-    mixed_rows = (
-        tracker.astype(jnp.float32)
-        + gamma_mix
-        * (
-            from_left.astype(jnp.float32)
-            + from_right.astype(jnp.float32)
-            - 2.0 * message.astype(jnp.float32)
-        )
-    ).astype(jnp.bfloat16)
-    _, mats, rows, columns = tracker.shape
-    owned_rows = lax.all_to_all(mixed_rows[0], "fsdp", split_axis=0, concat_axis=0, tiled=True)
-    result = orthogonalize(owned_rows.reshape(mats * rows, columns), columns)
+
+    def part(array, which):
+        return lax.dynamic_slice_in_dim(array, which * half, half, 0)
+
+    def within(array):
+        return lax.all_to_all(array, "fsdp", 0, 0, axis_index_groups=halves, tiled=True)
+
+    def gossip(piece):
+        return piece, shifted(piece, "rep", 1), shifted(piece, "rep", -1)
+
+    w = columns // 256 * 128
+    far_message, far_tracker = part(message, 1 - side), part(tracker, 1 - side)
+    g1 = gossip(far_message[..., :w])
+    g2 = gossip(far_message[..., w:])
+    g3 = gossip(part(message, side))
+    far1 = mix(far_tracker[..., :w], *g1)
+    _, g2 = lax.optimization_barrier((far1, g2))
+    far2 = mix(far_tracker[..., w:], *g2)
+    _, g3 = lax.optimization_barrier((far2, g3))
+    far1 = lax.ppermute(far1, "fsdp", far)
+    far2 = lax.ppermute(within(far2), "fsdp", far)
+    near = mix(part(tracker, side), *g3)
+    near, far1 = lax.optimization_barrier((near, far1))
+    merged = within(jnp.concatenate([near, far1], axis=-1))
+    near_rows = merged[..., :columns]
+    far_rows = jnp.concatenate([merged[..., columns:], far2], axis=-1)
+    owned = jnp.where(side == 0, jnp.concatenate([near_rows, far_rows], 0), jnp.concatenate([far_rows, near_rows], 0))
+    result = orthogonalize(owned.reshape(mats * rows, columns), columns)
     result = result.reshape(mats, rows, columns)
     return lax.all_to_all(result, "fsdp", split_axis=0, concat_axis=0, tiled=True)[None]
 

time: 118 us -> 107 us (0.907)
  blocking collectives: 74.2 us -> 37.3 us
  starting transfers between devices: 2.13 us -> 18.9 us
  other arithmetic: 4.6 us -> 8.85 us
  waiting for transfers between devices: 28.5 us -> 31.8 us
  local copies, waits for them, and re-layouts: 1.14 us -> 3.16 us
    all_to_all x1 -> x0, blocking collectives: 38.9 us -> none  [per_device(): lax.all_to_all(mixed_rows[0], 'fsdp', split_axis=0, concat_axis=0, tiled=...]
    all_to_all x0 -> x2, waiting for transfers between devices: none -> 18.5 us  [within(): lax.all_to_all(array, 'fsdp', 0, 0, axis_index_groups=halves, tiled=True)]
    ppermute x1 -> x3, waiting for transfers between devices: 28.5 us -> 13.3 us  [shifted(): return lax.ppermute(block, axis, route)]
    all_to_all x0 -> x2, starting transfers between devices: none -> 10.7 us  [within(): lax.all_to_all(array, 'fsdp', 0, 0, axis_index_groups=halves, tiled=True)]
    ppermute x0 -> x2, starting transfers between devices: none -> 4.52 us  [the longest x1 2.31 us: per_device(): far2 = lax.ppermute(within(far2), 'fsdp', far)]
    convert_element_type x0 -> x3, other arithmetic: none -> 4.24 us  [mix(): return (tracker.astype(f32) + gamma_mix * (left.astype(f32) + right.astyp...]
    all_to_all x1, blocking collectives: 35.3 us -> 37.3 us  [per_device(): lax.all_to_all(result, 'fsdp', split_axis=0, concat_axis=0, tiled=True)]
    ppermute x1 -> x3, starting transfers between devices: 2.13 us -> 3.67 us  [shifted(): return lax.ppermute(block, axis, route)]
  transfers between devices with their start and end apart: 1 -> 7, of which waited for: 1 -> 5; matrix products, arithmetic and copies ran while one was open for 0% -> 6% of each run, Pallas kernels for 0% -> 0%
where the time goes in v2:
time: 107 us
  blocking collectives  37.3 us (35%)
  waiting for transfers between devices  31.8 us (30%)
  starting transfers between devices  18.9 us (18%)
  other arithmetic  8.85 us (8%)
  matrix products  6.07 us (6%)
  local copies, waits for them, and re-layouts  3.16 us (3%)
    all_to_all x1, blocking collectives, per_device(): lax.all_to_all(result, 'fsdp', split_axis=0, concat_axis=0, tiled=True)  37.3 us
    all_to_all x2, waiting for transfers between devices, within(): lax.all_to_all(array, 'fsdp', 0, 0, axis_index_groups=halves, tiled=True)  18.5 us
    ppermute x3, waiting for transfers between devices, shifted(): return lax.ppermute(block, axis, route)  13.3 us
    all_to_all x2, starting transfers between devices, within(): lax.all_to_all(array, 'fsdp', 0, 0, axis_index_groups=halves, tiled=True)  10.7 us
    convert_element_type x3, other arithmetic, mix(): return (tracker.astype(f32) + gamma_mix * (left.astype(f32) + right.astyp...  4.24 us
    ppermute x3, starting transfers between devices, shifted(): return lax.ppermute(block, axis, route)  3.67 us
    dot_general x5, matrix products, orthogonalize(): jnp.dot(polynomial, iterate, preferred_element_type=jnp.float32)  3.47 us
    dot_general x5, matrix products, orthogonalize(): lax.dot_general(iterate, iterate, (((1,), (1,)), ((), ())), preferred_ele...  2.59 us
  transfers between devices with their start and end apart: 7, of which 5 were waited for; matrix products, arithmetic and copies ran while one was open for 6% of the time, Pallas kernels for 0%

profile of v2, /device:TPU:1, one launch (start us, length us, event | category | flops | bytes accessed | tf_op | source)
XLA Modules:
  0.0 106.9 jit_solution(779665560202389622)
XLA Ops:
  0.0 0.7 exponential_bitcast_fusion
  0.8 1.6 %fusion.11 = bf16[16,8,5120]{2,1,0:T(8,128)(2,1)S(1)} fusion(bf16[1,16,8,5120]{3,2,1,0:T(8,128)(2,1)} %param.4, f32[16,8]{1,0:T(8,128)S(1)} %copy.4), kind=kLoop, calls=%fused_computation.19 | loop fusion | flops 1966080 | bytes 2621952 | tf_op jit(solution)/shard_map/convert_element_type | solution.py:55
  2.5 2.1 %collective-permute-start = (bf16[8,8,2560]{2,1,0:T(8,128)(2,1)S(1)}, bf16[8,8,2560]{2,1,0:T(8,128)(2,1)}, u32[]{:S(2)}, u32[]{:S(2)}) collective-permute-start(bf16[8,8,2560]{2,1,0:T(8,128)(2,1)S(1)} %get-tuple-element.24), channel_id=1, source_target_pairs={{16,0},{0,16},{17,1},{1,17},{18,2},{2,18},{19,3},{3,19},{20,4},{4,... | collective-permute-start | bytes 983048 | tf_op jit(solution)/shard_map/ppermute | solution.py:17
  4.7 1.5 %collective-permute-start.2 = (bf16[8,8,5120]{2,1,0:T(8,128)(2,1)S(1)}, bf16[8,8,5120]{2,1,0:T(8,128)(2,1)S(1)}, u32[]{:S(2)}, u32[]{:S(2)}) collective-permute-start(bf16[8,8,5120]{2,1,0:T(8,128)(2,1)S(1)} %constant_dynamic-slice_fusion.1), channel_id=1, source_target_pairs={{16,0},{0,16},{17,1},{1,17},{18,2},{2,18},{19,3},{3,19},{20,4},{4,... | collective-permute-start | bytes 1966088 | tf_op jit(solution)/shard_map/ppermute | solution.py:17
  6.2 1.1 %dynamic-slice_bitcast_fusion = bf16[8,8,5120]{2,1,0:T(8,128)(2,1)S(1)} fusion(bf16[1,16,8,5120]{3,2,1,0:T(8,128)(2,1)} %param.3, s32[]{:T(128)S(6)} %select_n.38), kind=kLoop, calls=%fused_computation.47 | loop fusion | bytes 1310724 | tf_op jit(solution)/shard_map/dynamic_slice | solution.py:58
  7.3 4.8 %collective-permute-done = bf16[8,8,2560]{2,1,0:T(8,128)(2,1)} collective-permute-done((bf16[8,8,2560]{2,1,0:T(8,128)(2,1)S(1)}, bf16[8,8,2560]{2,1,0:T(8,128)(2,1)}, u32[]{:S(2)}, u32[]{:S(2)}) %collective-permute-start) | collective-permute-done | bytes 327712 | tf_op jit(solution)/shard_map/ppermute | solution.py:17
  12.1 1.9 %add_convert_fusion.1 = bf16[8,8,2560]{2,1,0:T(8,128)(2,1)} fusion(bf16[8,8,2560]{2,1,0:T(8,128)(2,1)S(1)} %get-tuple-element.24, bf16[8,8,2560]{2,1,0:T(8,128)(2,1)} %collective-permute-done, bf16[8,8,5120]{2,1,0:T(8,128)(2,1)S(1)} %dynamic-slice_bitcast_fusion), kind=kLoop, calls=%fused_computation.46 | loop fusion | flops 1474560 | bytes 1310720 | tf_op jit(solution)/shard_map/convert_element_type | solution.py:25
  14.0 2.2 %collective-permute-start.3 = (bf16[8,8,2560]{2,1,0:T(8,128)(2,1)}, bf16[8,8,2560]{2,1,0:T(8,128)(2,1)S(1)}, u32[]{:S(2)}, u32[]{:S(2)}) collective-permute-start(bf16[8,8,2560]{2,1,0:T(8,128)(2,1)} %add_convert_fusion.1), channel_id=1, source_target_pairs={{0,8},{1,9},{2,10},{3,11},{4,12},{5,13},{6,14},{7,15},{8,0},{9,1},... | collective-permute-start | bytes 983048 | tf_op jit(solution)/shard_map/ppermute | solution.py:75
  16.2 2.9 %collective-permute-done.1 = bf16[8,8,2560]{2,1,0:T(8,128)(2,1)} collective-permute-done((bf16[8,8,2560]{2,1,0:T(8,128)(2,1)S(1)}, bf16[8,8,2560]{2,1,0:T(8,128)(2,1)}, u32[]{:S(2)}, u32[]{:S(2)}) %collective-permute-start.1) | collective-permute-done | bytes 327712 | tf_op jit(solution)/shard_map/ppermute | solution.py:17
  19.2 2.0 %add_convert_fusion = bf16[8,8,2560]{2,1,0:T(8,128)(2,1)} fusion(bf16[8,8,2560]{2,1,0:T(8,128)(2,1)S(1)} %get-tuple-element.15, bf16[8,8,2560]{2,1,0:T(8,128)(2,1)} %collective-permute-done.1, bf16[8,8,5120]{2,1,0:T(8,128)(2,1)S(1)} %dynamic-slice_bitcast_fusion), kind=kLoop, calls=%fused_computation.45 | loop fusion | flops 1638400 | bytes 1310720 | tf_op jit(solution)/shard_map/convert_element_type | solution.py:25
  21.2 6.4 %all-to-all-start.1 = ((bf16[8,8,2560]{2,1,0:T(8,128)(2,1)}), bf16[8,8,2560]{2,1,0:T(8,128)(2,1)S(1)}, u32[]{:S(2)}, u32[]{:S(2)}) async-start(bf16[8,8,2560]{2,1,0:T(8,128)(2,1)} %add_convert_fusion), calls=%async_computation.1 | async-start | bytes 655360 | tf_op jit(solution)/shard_map/all_to_all | solution.py:61
  27.5 5.6 %collective-permute-done.2 = bf16[8,8,5120]{2,1,0:T(8,128)(2,1)S(1)} collective-permute-done((bf16[8,8,5120]{2,1,0:T(8,128)(2,1)S(1)}, bf16[8,8,5120]{2,1,0:T(8,128)(2,1)S(1)}, u32[]{:S(2)}, u32[]{:S(2)}) %collective-permute-start.2) | collective-permute-done | bytes 655392 | tf_op jit(solution)/shard_map/ppermute | solution.py:17
  33.1 0.4 fusion.13
  33.5 1.0 pad_maximum_fusion
  34.5 0.9 all-to-all-done.1
  35.3 0.7 copy-done.1
  36.1 4.4 %all-to-all-start = ((bf16[8,8,7680]{2,1,0:T(8,128)(2,1)}), bf16[8,8,7680]{2,1,0:T(8,128)(2,1)S(1)}, u32[]{:S(2)}, u32[]{:S(2)}) async-start(bf16[8,8,7680]{2,1,0:T(8,128)(2,1)} %pad_maximum_fusion), calls=%async_computation | async-start | bytes 1966080 | tf_op jit(solution)/shard_map/all_to_all | solution.py:61
  40.4 2.3 %collective-permute-start.4 = (bf16[8,8,2560]{2,1,0:T(8,128)(2,1)}, bf16[8,8,2560]{2,1,0:T(8,128)(2,1)S(1)}, u32[]{:S(2)}, u32[]{:S(2)}) collective-permute-start(bf16[8,8,2560]{2,1,0:T(8,128)(2,1)} %copy-done.1), channel_id=1, source_target_pairs={{0,8},{1,9},{2,10},{3,11},{4,12},{5,13},{6,14},{7,15},{8,0},{9,1},... | collective-permute-start | bytes 983048 | tf_op jit(solution)/shard_map/ppermute | solution.py:76
  42.8 17.6 %all-to-all-done = bf16[8,8,7680]{2,1,0:T(8,128)(2,1)S(1)} async-done(((bf16[8,8,7680]{2,1,0:T(8,128)(2,1)}), bf16[8,8,7680]{2,1,0:T(8,128)(2,1)S(1)}, u32[]{:S(2)}, u32[]{:S(2)}) %all-to-all-start) | async-done | bytes 983072 | tf_op jit(solution)/shard_map/all_to_all | solution.py:61
  60.4 1.3 %fusion.9 = (f32[]{:T(128)}, bf16[16,8,5120]{2,1,0:T(8,128)(2,1)S(1)}) fusion(bf16[8,8,5120]{2,1,0:T(8,128)(2,1)S(1)} %slice.26, bf16[8,8,2560]{2,1,0:T(8,128)(2,1)S(1)} %collective-permute-done.4, bf16[8,8,2560]{2,1,0:T(8,128)(2,1)S(1)} %slice.27, pred[]{:T(512)S(6)} %eq.3), kind=kLoop, calls=%fused_computation.16 | loop fusion | flops 10485759 | bytes 2621445 | tf_op jit(solution)/shard_map/reduce_sum | solution.py:30
  62.4 0.6 convolution_convert_fusion.4
  63.0 0.8 fusion
  63.8 0.5 convolution_convert_fusion.3
  64.4 0.6 fusion.1
  65.0 0.5 convolution_convert_fusion.2
  65.5 0.6 fusion.2
  66.1 0.5 convolution_convert_fusion.1
  66.7 0.6 fusion.3
  67.3 0.5 convolution_convert_fusion
  67.8 0.7 fusion.8
  68.6 37.3 %all_to_all.15 = bf16[16,8,5120]{2,1,0:T(8,128)(2,1)S(1)} all-to-all(bf16[16,8,5120]{2,1,0:T(8,128)(2,1)S(1)} %fusion.8), channel_id=1, replica_groups=mesh['rep'=2,'fsdp'=16] {'fsdp'}, dimensions={0} | all-to-all | bytes 2621440 | tf_op jit(solution)/shard_map/all_to_all | solution.py:85
  105.9 1.1 copy.6
  (11 shorter events, 0.3 us)
Async XLA Ops:
  2.5 9.7 %collective-permute-start = (bf16[8,8,2560]{2,1,0:T(8,128)(2,1)S(1)}, bf16[8,8,2560]{2,1,0:T(8,128)(2,1)}, u32[]{:S(2)}, u32[]{:S(2)}) collective-permute-start(bf16[8,8,2560]{2,1,0:T(8,128)(2,1)S(1)} %get-tuple-element.24), channel_id=1, source_target_pairs={{16,0},{0,16},{17,1},{1,17},{18,2},{2,18},{19,3},{3,19},{20,4},{4,... | collective-permute-start | bytes 983048 | tf_op jit(solution)/shard_map/ppermute | solution.py:17
  4.6 14.6 %collective-permute-start.1 = (bf16[8,8,2560]{2,1,0:T(8,128)(2,1)S(1)}, bf16[8,8,2560]{2,1,0:T(8,128)(2,1)}, u32[]{:S(2)}, u32[]{:S(2)}) collective-permute-start(bf16[8,8,2560]{2,1,0:T(8,128)(2,1)S(1)} %get-tuple-element.15), channel_id=1, source_target_pairs={{16,0},{0,16},{17,1},{1,17},{18,2},{2,18},{19,3},{3,19},{20,4},{4,... | collective-permute-start | bytes 983048 | tf_op jit(solution)/shard_map/ppermute | solution.py:17
  4.7 28.4 %collective-permute-start.2 = (bf16[8,8,5120]{2,1,0:T(8,128)(2,1)S(1)}, bf16[8,8,5120]{2,1,0:T(8,128)(2,1)S(1)}, u32[]{:S(2)}, u32[]{:S(2)}) collective-permute-start(bf16[8,8,5120]{2,1,0:T(8,128)(2,1)S(1)} %constant_dynamic-slice_fusion.1), channel_id=1, source_target_pairs={{16,0},{0,16},{17,1},{1,17},{18,2},{2,18},{19,3},{3,19},{20,4},{4,... | collective-permute-start | bytes 1966088 | tf_op jit(solution)/shard_map/ppermute | solution.py:17
  14.0 19.1 %copy-start = (bf16[1,16,8,5120]{3,2,1,0:T(8,128)(2,1)S(1)}, bf16[1,16,8,5120]{3,2,1,0:T(8,128)(2,1)}, u32[]{:S(2)}) copy-start(bf16[1,16,8,5120]{3,2,1,0:T(8,128)(2,1)} %param.3) | copy-start | bytes 3932164
  14.0 19.5 %collective-permute-start.3 = (bf16[8,8,2560]{2,1,0:T(8,128)(2,1)}, bf16[8,8,2560]{2,1,0:T(8,128)(2,1)S(1)}, u32[]{:S(2)}, u32[]{:S(2)}) collective-permute-start(bf16[8,8,2560]{2,1,0:T(8,128)(2,1)} %add_convert_fusion.1), channel_id=1, source_target_pairs={{0,8},{1,9},{2,10},{3,11},{4,12},{5,13},{6,14},{7,15},{8,0},{9,1},... | collective-permute-start | bytes 983048 | tf_op jit(solution)/shard_map/ppermute | solution.py:75
  21.2 14.2 %all-to-all-start.1 = ((bf16[8,8,2560]{2,1,0:T(8,128)(2,1)}), bf16[8,8,2560]{2,1,0:T(8,128)(2,1)S(1)}, u32[]{:S(2)}, u32[]{:S(2)}) async-start(bf16[8,8,2560]{2,1,0:T(8,128)(2,1)} %add_convert_fusion), calls=%async_computation.1 | async-start | bytes 655360 | tf_op jit(solution)/shard_map/all_to_all | solution.py:61
  35.3 0.7 copy-start.1
  36.1 24.3 %all-to-all-start = ((bf16[8,8,7680]{2,1,0:T(8,128)(2,1)}), bf16[8,8,7680]{2,1,0:T(8,128)(2,1)S(1)}, u32[]{:S(2)}, u32[]{:S(2)}) async-start(bf16[8,8,7680]{2,1,0:T(8,128)(2,1)} %pad_maximum_fusion), calls=%async_computation | async-start | bytes 1966080 | tf_op jit(solution)/shard_map/all_to_all | solution.py:61
  40.4 20.0 %collective-permute-start.4 = (bf16[8,8,2560]{2,1,0:T(8,128)(2,1)}, bf16[8,8,2560]{2,1,0:T(8,128)(2,1)S(1)}, u32[]{:S(2)}, u32[]{:S(2)}) collective-permute-start(bf16[8,8,2560]{2,1,0:T(8,128)(2,1)} %copy-done.1), channel_id=1, source_target_pairs={{0,8},{1,9},{2,10},{3,11},{4,12},{5,13},{6,14},{7,15},{8,0},{9,1},... | collective-permute-start | bytes 983048 | tf_op jit(solution)/shard_map/ppermute | solution.py:76

commit v3 on v2

v3 whole, which is shorter than its diff:
```python
import math
import jax
import jax.numpy as jnp
from jax import lax
from jax.sharding import PartitionSpec as P

NS_STEPS = 5
gamma_mix = 0.5
coef_a = 3.4445
coef_b = -4.775
coef_c = 2.0315


def shifted(block, axis, distance):
    devices = range(lax.axis_size(axis))
    route = [((i - distance) % len(devices), i) for i in devices]
    return lax.ppermute(block, axis, route)


def mix(tracker, message, left, right):
    f32 = jnp.float32
    return (
        tracker.astype(f32)
        + gamma_mix * (left.astype(f32) + right.astype(f32) - 2.0 * message.astype(f32))
    ).astype(jnp.bfloat16)


def orthogonalize(matrix, order, rows, columns):
    f32 = jnp.float32
    factor = 2.0 ** (int(math.log2(columns)) // 2)
    eye = jnp.eye(matrix.shape[0], dtype=f32)
    iterate = matrix
    for iteration in range(NS_STEPS):
        last = iteration == NS_STEPS - 1
        gram = lax.dot_general(iterate, iterate, (((1,), (1,)), ((), ())), preferred_element_type=f32)
        scale = 1.0
        if iteration == 0:
            gram = lax.optimization_barrier(gram)
            trace = jnp.broadcast_to(jnp.sum(gram * eye, axis=0, keepdims=True), (rows, gram.shape[1]))
            trace = jnp.sum(lax.optimization_barrier(trace), axis=1, keepdims=True)
            scale = jnp.tile(1.0 / (jnp.sqrt(trace) + 1e-07), (gram.shape[0] // rows, 1))
            gram = gram * (scale * scale)
        gram = gram.astype(jnp.bfloat16)
        square = jnp.dot(gram, gram, preferred_element_type=f32)
        polynomial = coef_b * gram.astype(f32) + coef_c * square
        if last:
            polynomial = order((coef_a * eye + polynomial) * factor).astype(jnp.bfloat16)
            return jnp.dot(polynomial, iterate, preferred_element_type=f32).astype(jnp.bfloat16)
        product = jnp.dot(polynomial.astype(jnp.bfloat16), iterate, preferred_element_type=f32)
        iterate = ((coef_a * iterate.astype(f32) + product) * scale).astype(jnp.bfloat16)


def per_device(tracker, levels, exponents):
    tracker, levels, exponents = tracker[0], levels[0], exponents[0]
    mats, rows, columns = tracker.shape
    half = mats // 2
    side = lax.axis_index("fsdp") // half
    halves = [list(range(half)), list(range(half, mats))]
    far = [(i, (i + half) % mats) for i in range(mats)]

    powers = jnp.exp2(exponents.astype(jnp.float32))[..., None]

    def dequantized(block, scale):
        return (block.astype(jnp.float32) * scale).astype(jnp.bfloat16)

    def part(array, which):
        return lax.dynamic_slice_in_dim(array, which * half, half, 0)

    def within(array):
        return lax.all_to_all(array, "fsdp", 0, 0, axis_index_groups=halves, tiled=True)

    def gossip(piece):
        return piece, shifted(piece, "rep", 1), shifted(piece, "rep", -1)

    w = columns // 256 * 128
    far_tracker1, far_tracker2 = part(tracker, 1 - side)[..., :w], part(tracker, 1 - side)[..., w:]
    near_tracker = part(tracker, side)
    far_powers = part(powers, 1 - side)
    message1 = dequantized(part(levels, 1 - side)[..., :w], far_powers)
    message1, levels = lax.optimization_barrier((message1, levels))
    message2 = dequantized(part(levels, 1 - side)[..., w:], far_powers)
    message3 = dequantized(part(levels, side), part(powers, side))
    far_tracker1, far_tracker2, near_tracker = lax.optimization_barrier((far_tracker1, far_tracker2, near_tracker))
    g1, g2, g3 = gossip(message1), gossip(message2), gossip(message3)
    far1 = mix(far_tracker1, *g1)
    _, g2 = lax.optimization_barrier((far1, g2))
    far2 = mix(far_tracker2, *g2)
    _, g3 = lax.optimization_barrier((far2, g3))
    far1 = lax.ppermute(far1, "fsdp", far)
    far2 = lax.ppermute(within(far2), "fsdp", far)
    near = mix(near_tracker, *g3)
    near, far1 = lax.optimization_barrier((near, far1))
    merged = within(jnp.concatenate([near, far1], axis=-1))
    near_rows = merged[..., :columns]
    far_rows = jnp.concatenate([merged[..., columns:], far2], axis=-1)
    owned = jnp.concatenate([near_rows, far_rows], 0).reshape(mats * rows, columns)
    owned = lax.optimization_barrier(owned)

    def order(square):
        return jnp.where(side == 0, square, jnp.roll(square, half * rows, axis=0))

    result = orthogonalize(owned, order, rows, columns)
    result = result.reshape(mats, rows, columns)
    return lax.all_to_all(result, "fsdp", split_axis=0, concat_axis=0, tiled=True)[None]


def solution(mesh):
    in_specs = (P("rep", None, "fsdp", None), P("rep", None, "fsdp", None), P("rep", None, "fsdp"))
    out_specs = P("rep", None, "fsdp", None)
    return jax.shard_map(
        per_device, mesh=mesh, in_specs=in_specs, out_specs=out_specs, check_vma=False
    )
```

time: 107 us -> 105 us (0.981)
  other arithmetic: 8.85 us -> 3.9 us
  local copies, waits for them, and re-layouts: 3.16 us -> 4.66 us
    convert_element_type x3, other arithmetic: 4.24 us -> 2.18 us  [mix(): return (tracker.astype(f32) + gamma_mix * (left.astype(f32) + right.astyp...]
    ppermute x3, waiting for transfers between devices: 13.3 us -> 14.8 us  [shifted(): return lax.ppermute(block, axis, route)]
    dynamic_slice x2, local copies, waits for them, and re-layouts: 1.17 us -> 2.5 us  [part(): return lax.dynamic_slice_in_dim(array, which * half, half, 0)]
    convert_element_type x1 -> x3, other arithmetic: 1.62 us -> 0.42 us  [dequantized(): return (block.astype(jnp.float32) * scale).astype(jnp.bfloat16)]
    reduce_sum x1 -> x2, other arithmetic: 1.29 us -> 0.15 us  [the longest x1 0.12 us: orthogonalize(): trace = jnp.sum(lax.optimization_barrier(trace), axis=1, keepdims=True)]
    dot_general x5 -> x6, matrix products: 3.47 us -> 3.34 us  [the longest x4 2.7 us: orthogonalize(): jnp.dot(polynomial.astype(jnp.bfloat16), iterate, preferred_element_type=...]
  transfers between devices with their start and end apart: 7 -> 7, of which waited for: 5 -> 4; matrix products, arithmetic and copies ran while one was open for 6% -> 5% of each run, Pallas kernels for 0% -> 0%
where the time goes in v3:
time: 105 us; the launch traced here: 104 us
  blocking collectives  37.3 us (36%)
  waiting for transfers between devices  32.4 us (31%)
  starting transfers between devices  19.8 us (19%)
  matrix products  5.86 us (6%)
  local copies, waits for them, and re-layouts  4.66 us (4%)
  other arithmetic  3.9 us (4%)
    all_to_all x1, blocking collectives, per_device(): lax.all_to_all(result, 'fsdp', split_axis=0, concat_axis=0, tiled=True)  37.3 us
    all_to_all x2, waiting for transfers between devices, within(): lax.all_to_all(array, 'fsdp', 0, 0, axis_index_groups=halves, tiled=True)  17.6 us
    ppermute x3, waiting for transfers between devices, shifted(): return lax.ppermute(block, axis, route)  14.8 us
    all_to_all x2, starting transfers between devices, within(): lax.all_to_all(array, 'fsdp', 0, 0, axis_index_groups=halves, tiled=True)  11.6 us
    ppermute x3, starting transfers between devices, shifted(): return lax.ppermute(block, axis, route)  3.73 us
    dot_general x4, matrix products, orthogonalize(): jnp.dot(polynomial.astype(jnp.bfloat16), iterate, preferred_element_type=...  2.7 us
    dot_general x5, matrix products, orthogonalize(): lax.dot_general(iterate, iterate, (((1,), (1,)), ((), ())), preferred_ele...  2.52 us
    dynamic_slice x2, local copies, waits for them, and re-layouts, part(): return lax.dynamic_slice_in_dim(array, which * half, half, 0)  2.5 us
  transfers between devices with their start and end apart: 7, of which 4 were waited for; matrix products, arithmetic and copies ran while one was open for 5% of the time, Pallas kernels for 0%

profile of v3, /device:TPU:1, one launch (start us, length us, event | category | flops | bytes accessed | tf_op | source)
XLA Modules:
  0.0 104.2 jit_solution(17514165561952314233)
XLA Ops:
  0.0 0.9 copy.5
  0.9 1.1 %dynamic-slice_bitcast_fusion = bf16[8,8,5120]{2,1,0:T(8,128)(2,1)S(1)} fusion(bf16[1,16,8,5120]{3,2,1,0:T(8,128)(2,1)} %param.4, s32[]{:T(128)S(6)} %select_n.27), kind=kLoop, calls=%fused_computation.39 | loop fusion | bytes 1310724 | tf_op jit(solution)/shard_map/dynamic_slice | solution.py:67
  2.0 0.1 multiply_convert_fusion.2
  2.2 2.1 %collective-permute-start = (bf16[8,8,2560]{2,1,0:T(8,128)(2,1)S(1)}, bf16[8,8,2560]{2,1,0:T(8,128)(2,1)S(1)}, u32[]{:S(2)}, u32[]{:S(2)}) collective-permute-start(bf16[8,8,2560]{2,1,0:T(8,128)(2,1)S(1)} %multiply_convert_fusion.2), channel_id=1, source_target_pairs={{16,0},{0,16},{17,1},{1,17},{18,2},{2,18},{19,3},{3,19},{20,4},{4,... | collective-permute-start | bytes 983048 | tf_op jit(solution)/shard_map/ppermute | solution.py:17
  4.5 0.2 multiply_convert_fusion
  4.7 1.5 %collective-permute-start.2 = (bf16[8,8,5120]{2,1,0:T(8,128)(2,1)S(1)}, bf16[8,8,5120]{2,1,0:T(8,128)(2,1)S(1)}, u32[]{:S(2)}, u32[]{:S(2)}) collective-permute-start(bf16[8,8,5120]{2,1,0:T(8,128)(2,1)S(1)} %multiply_convert_fusion), channel_id=1, source_target_pairs={{16,0},{0,16},{17,1},{1,17},{18,2},{2,18},{19,3},{3,19},{20,4},{4,... | collective-permute-start | bytes 1966088 | tf_op jit(solution)/shard_map/ppermute | solution.py:17
  6.2 1.4 %dynamic-slice_bitcast_fusion.1 = (bf16[8,8,5120]{2,1,0:T(8,128)(2,1)S(1)}, bf16[8,8,5120]{2,1,0:T(8,128)(2,1)S(1)}) fusion(bf16[1,16,8,5120]{3,2,1,0:T(8,128)(2,1)} %param.3, s32[]{:T(128)S(6)} %select_n.28, s32[]{:T(128)S(6)} %select_n.27), kind=kLoop, calls=%fused_computation.40 | loop fusion | bytes 2621448 | tf_op jit(solution)/shard_map/dynamic_slice | solution.py:67
  7.6 4.1 %collective-permute-done = bf16[8,8,2560]{2,1,0:T(8,128)(2,1)S(1)} collective-permute-done((bf16[8,8,2560]{2,1,0:T(8,128)(2,1)S(1)}, bf16[8,8,2560]{2,1,0:T(8,128)(2,1)S(1)}, u32[]{:S(2)}, u32[]{:S(2)}) %collective-permute-start) | collective-permute-done | bytes 327712 | tf_op jit(solution)/shard_map/ppermute | solution.py:17
  11.7 0.9 add_convert_fusion.2
  12.6 2.2 %collective-permute-start.3 = (bf16[8,8,2560]{2,1,0:T(8,128)(2,1)}, bf16[8,8,2560]{2,1,0:T(8,128)(2,1)S(1)}, u32[]{:S(2)}, u32[]{:S(2)}) collective-permute-start(bf16[8,8,2560]{2,1,0:T(8,128)(2,1)} %add_convert_fusion.2), channel_id=1, source_target_pairs={{0,8},{1,9},{2,10},{3,11},{4,12},{5,13},{6,14},{7,15},{8,0},{9,1},... | collective-permute-start | bytes 983048 | tf_op jit(solution)/shard_map/ppermute | solution.py:89
  14.9 3.9 %collective-permute-done.1 = bf16[8,8,2560]{2,1,0:T(8,128)(2,1)S(1)} collective-permute-done((bf16[8,8,2560]{2,1,0:T(8,128)(2,1)S(1)}, bf16[8,8,2560]{2,1,0:T(8,128)(2,1)S(1)}, u32[]{:S(2)}, u32[]{:S(2)}) %collective-permute-start.1) | collective-permute-done | bytes 327712 | tf_op jit(solution)/shard_map/ppermute | solution.py:17
  18.8 0.9 add_convert_fusion.1
  19.7 6.4 %all-to-all-start.1 = ((bf16[8,8,2560]{2,1,0:T(8,128)(2,1)}), bf16[8,8,2560]{2,1,0:T(8,128)(2,1)S(1)}, u32[]{:S(2)}, u32[]{:S(2)}) async-start(bf16[8,8,2560]{2,1,0:T(8,128)(2,1)} %add_convert_fusion.1), calls=%async_computation.1 | async-start | bytes 655360 | tf_op jit(solution)/shard_map/all_to_all | solution.py:70
  26.0 6.8 %collective-permute-done.2 = bf16[8,8,5120]{2,1,0:T(8,128)(2,1)S(1)} collective-permute-done((bf16[8,8,5120]{2,1,0:T(8,128)(2,1)S(1)}, bf16[8,8,5120]{2,1,0:T(8,128)(2,1)S(1)}, u32[]{:S(2)}, u32[]{:S(2)}) %collective-permute-start.2) | collective-permute-done | bytes 655392 | tf_op jit(solution)/shard_map/ppermute | solution.py:17
  32.8 0.4 add_convert_fusion
  33.2 1.0 pad_maximum_fusion
  34.2 5.2 %all-to-all-start = ((bf16[8,8,7680]{2,1,0:T(8,128)(2,1)}), bf16[8,8,7680]{2,1,0:T(8,128)(2,1)S(1)}, u32[]{:S(2)}, u32[]{:S(2)}) async-start(bf16[8,8,7680]{2,1,0:T(8,128)(2,1)} %pad_maximum_fusion), calls=%async_computation | async-start | bytes 1966080 | tf_op jit(solution)/shard_map/all_to_all | solution.py:70
  39.4 2.3 %collective-permute-start.4 = (bf16[8,8,2560]{2,1,0:T(8,128)(2,1)S(1)}, bf16[8,8,2560]{2,1,0:T(8,128)(2,1)S(1)}, u32[]{:S(2)}, u32[]{:S(2)}) collective-permute-start(bf16[8,8,2560]{2,1,0:T(8,128)(2,1)S(1)} %all-to-all-done.1), channel_id=1, source_target_pairs={{0,8},{1,9},{2,10},{3,11},{4,12},{5,13},{6,14},{7,15},{8,0},{9,1},... | collective-permute-start | bytes 983048 | tf_op jit(solution)/shard_map/ppermute | solution.py:90
  41.7 17.6 %all-to-all-done = bf16[8,8,7680]{2,1,0:T(8,128)(2,1)S(1)} async-done(((bf16[8,8,7680]{2,1,0:T(8,128)(2,1)}), bf16[8,8,7680]{2,1,0:T(8,128)(2,1)S(1)}, u32[]{:S(2)}, u32[]{:S(2)}) %all-to-all-start) | async-done | bytes 983072 | tf_op jit(solution)/shard_map/all_to_all | solution.py:70
  59.5 0.5 fusion.49
  60.4 0.8 fusion.4
  61.2 0.5 convolution_convert_fusion.4
  61.7 0.6 fusion.1
  62.3 0.5 convolution_convert_fusion.3
  62.8 0.6 fusion.2
  63.5 0.5 convolution_convert_fusion.2
  64.0 0.6 fusion.3
  64.6 0.5 convolution_convert_fusion.1
  65.1 0.1 fusion.8
  65.3 0.5 fusion.5
  65.8 37.3 %all_to_all.15 = bf16[16,8,5120]{2,1,0:T(8,128)(2,1)S(1)} all-to-all(bf16[16,8,5120]{2,1,0:T(8,128)(2,1)S(1)} %fusion.5), channel_id=1, replica_groups=mesh['rep'=2,'fsdp'=16] {'fsdp'}, dimensions={0} | all-to-all | bytes 2621440 | tf_op jit(solution)/shard_map/all_to_all | solution.py:104
  103.1 1.1 %copy.7 = bf16[1,16,8,5120]{3,2,1,0:T(8,128)(2,1)} copy(bf16[1,16,8,5120]{3,2,1,0:T(8,128)(2,1)S(1)} %bitcast.39) | data formatting | bytes 2621440
  (21 shorter events, 0.8 us)
Async XLA Ops:
  0.0 4.3 %copy-start = (bf16[1,16,8,5120]{3,2,1,0:T(8,128)(2,1)S(1)}, bf16[1,16,8,5120]{3,2,1,0:T(8,128)(2,1)}, u32[]{:S(2)}) copy-start(bf16[1,16,8,5120]{3,2,1,0:T(8,128)(2,1)} %param.4) | copy-start | bytes 3932164
  2.2 9.6 %collective-permute-start = (bf16[8,8,2560]{2,1,0:T(8,128)(2,1)S(1)}, bf16[8,8,2560]{2,1,0:T(8,128)(2,1)S(1)}, u32[]{:S(2)}, u32[]{:S(2)}) collective-permute-start(bf16[8,8,2560]{2,1,0:T(8,128)(2,1)S(1)} %multiply_convert_fusion.2), channel_id=1, source_target_pairs={{16,0},{0,16},{17,1},{1,17},{18,2},{2,18},{19,3},{3,19},{20,4},{4,... | collective-permute-start | bytes 983048 | tf_op jit(solution)/shard_map/ppermute | solution.py:17
  4.4 14.3 %collective-permute-start.1 = (bf16[8,8,2560]{2,1,0:T(8,128)(2,1)S(1)}, bf16[8,8,2560]{2,1,0:T(8,128)(2,1)S(1)}, u32[]{:S(2)}, u32[]{:S(2)}) collective-permute-start(bf16[8,8,2560]{2,1,0:T(8,128)(2,1)S(1)} %multiply_convert_fusion.1), channel_id=1, source_target_pairs={{16,0},{0,16},{17,1},{1,17},{18,2},{2,18},{19,3},{3,19},{20,4},{4,... | collective-permute-start | bytes 983048 | tf_op jit(solution)/shard_map/ppermute | solution.py:17
  4.7 28.1 %collective-permute-start.2 = (bf16[8,8,5120]{2,1,0:T(8,128)(2,1)S(1)}, bf16[8,8,5120]{2,1,0:T(8,128)(2,1)S(1)}, u32[]{:S(2)}, u32[]{:S(2)}) collective-permute-start(bf16[8,8,5120]{2,1,0:T(8,128)(2,1)S(1)} %multiply_convert_fusion), channel_id=1, source_target_pairs={{16,0},{0,16},{17,1},{1,17},{18,2},{2,18},{19,3},{3,19},{20,4},{4,... | collective-permute-start | bytes 1966088 | tf_op jit(solution)/shard_map/ppermute | solution.py:17
  12.6 20.5 %collective-permute-start.3 = (bf16[8,8,2560]{2,1,0:T(8,128)(2,1)}, bf16[8,8,2560]{2,1,0:T(8,128)(2,1)S(1)}, u32[]{:S(2)}, u32[]{:S(2)}) collective-permute-start(bf16[8,8,2560]{2,1,0:T(8,128)(2,1)} %add_convert_fusion.2), channel_id=1, source_target_pairs={{0,8},{1,9},{2,10},{3,11},{4,12},{5,13},{6,14},{7,15},{8,0},{9,1},... | collective-permute-start | bytes 983048 | tf_op jit(solution)/shard_map/ppermute | solution.py:89
  19.7 14.5 %all-to-all-start.1 = ((bf16[8,8,2560]{2,1,0:T(8,128)(2,1)}), bf16[8,8,2560]{2,1,0:T(8,128)(2,1)S(1)}, u32[]{:S(2)}, u32[]{:S(2)}) async-start(bf16[8,8,2560]{2,1,0:T(8,128)(2,1)} %add_convert_fusion.1), calls=%async_computation.1 | async-start | bytes 655360 | tf_op jit(solution)/shard_map/all_to_all | solution.py:70
  34.2 25.1 %all-to-all-start = ((bf16[8,8,7680]{2,1,0:T(8,128)(2,1)}), bf16[8,8,7680]{2,1,0:T(8,128)(2,1)S(1)}, u32[]{:S(2)}, u32[]{:S(2)}) async-start(bf16[8,8,7680]{2,1,0:T(8,128)(2,1)} %pad_maximum_fusion), calls=%async_computation | async-start | bytes 1966080 | tf_op jit(solution)/shard_map/all_to_all | solution.py:70
  39.4 20.0 %collective-permute-start.4 = (bf16[8,8,2560]{2,1,0:T(8,128)(2,1)S(1)}, bf16[8,8,2560]{2,1,0:T(8,128)(2,1)S(1)}, u32[]{:S(2)}, u32[]{:S(2)}) collective-permute-start(bf16[8,8,2560]{2,1,0:T(8,128)(2,1)S(1)} %all-to-all-done.1), channel_id=1, source_target_pairs={{0,8},{1,9},{2,10},{3,11},{4,12},{5,13},{6,14},{7,15},{8,0},{9,1},... | collective-permute-start | bytes 983048 | tf_op jit(solution)/shard_map/ppermute | solution.py:90

commit v4 on v3

--- a/solution.py
+++ b/solution.py
@@ -2,6 +2,8 @@
 import jax
 import jax.numpy as jnp
 from jax import lax
+from jax.experimental import pallas as pl
+from jax.experimental.pallas import tpu as pltpu
 from jax.sharding import PartitionSpec as P
 
 NS_STEPS = 5
@@ -23,6 +25,21 @@
         tracker.astype(f32)
         + gamma_mix * (left.astype(f32) + right.astype(f32) - 2.0 * message.astype(f32))
     ).astype(jnp.bfloat16)
+
+
+def copy_kernel(block_ref, out_ref):
+    out_ref[...] = block_ref[...]
+
+
+def settle(block, flops):
+    spec = pl.BlockSpec(memory_space=pltpu.VMEM)
+    return pl.pallas_call(
+        copy_kernel,
+        out_shape=jax.ShapeDtypeStruct(block.shape, block.dtype),
+        in_specs=[spec],
+        out_specs=spec,
+        cost_estimate=pl.CostEstimate(flops=flops, bytes_accessed=0, transcendentals=0),
+    )(block)
 
 
 def orthogonalize(matrix, order, rows, columns):
@@ -56,7 +73,11 @@
     half = mats // 2
     side = lax.axis_index("fsdp") // half
     halves = [list(range(half)), list(range(half, mats))]
-    far = [(i, (i + half) % mats) for i in range(mats)]
+    far = [(i, i ^ (half + half // 2)) for i in range(mats)]
+
+    def mirrored(block):
+        return jnp.concatenate([block[half // 2 :], block[: half // 2]], 0)
+
 
     powers = jnp.exp2(exponents.astype(jnp.float32))[..., None]
 
@@ -72,13 +93,13 @@
     def gossip(piece):
         return piece, shifted(piece, "rep", 1), shifted(piece, "rep", -1)
 
-    w = columns // 256 * 128
-    far_tracker1, far_tracker2 = part(tracker, 1 - side)[..., :w], part(tracker, 1 - side)[..., w:]
+    w = columns * 13 // 20 // 128 * 128
+    far_tracker1, far_tracker2 = part(tracker, 1 - side)[..., :w], mirrored(part(tracker, 1 - side)[..., w:])
     near_tracker = part(tracker, side)
     far_powers = part(powers, 1 - side)
     message1 = dequantized(part(levels, 1 - side)[..., :w], far_powers)
     message1, levels = lax.optimization_barrier((message1, levels))
-    message2 = dequantized(part(levels, 1 - side)[..., w:], far_powers)
+    message2 = dequantized(mirrored(part(levels, 1 - side)[..., w:]), mirrored(far_powers))
     message3 = dequantized(part(levels, side), part(powers, side))
     far_tracker1, far_tracker2, near_tracker = lax.optimization_barrier((far_tracker1, far_tracker2, near_tracker))
     g1, g2, g3 = gossip(message1), gossip(message2), gossip(message3)
@@ -87,12 +108,12 @@
     far2 = mix(far_tracker2, *g2)
     _, g3 = lax.optimization_barrier((far2, g3))
     far1 = lax.ppermute(far1, "fsdp", far)
-    far2 = lax.ppermute(within(far2), "fsdp", far)
+    far2 = settle(lax.ppermute(within(far2), "fsdp", far), 20000000000)
     near = mix(near_tracker, *g3)
     near, far1 = lax.optimization_barrier((near, far1))
     merged = within(jnp.concatenate([near, far1], axis=-1))
     near_rows = merged[..., :columns]
-    far_rows = jnp.concatenate([merged[..., columns:], far2], axis=-1)
+    far_rows = jnp.concatenate([mirrored(merged[..., columns:]), far2], axis=-1)
     owned = jnp.concatenate([near_rows, far_rows], 0).reshape(mats * rows, columns)
     owned = lax.optimization_barrier(owned)
 

time: 105 us -> 100 us (0.952)
  waiting for transfers between devices: 32.4 us -> 25.3 us
  starting transfers between devices: 19.8 us -> 21.9 us
  blocking collectives: 37.3 us -> 35.3 us
  Pallas kernels: 0 us -> 1.64 us
    all_to_all x2, waiting for transfers between devices: 17.6 us -> 11.6 us  [within(): lax.all_to_all(array, 'fsdp', 0, 0, axis_index_groups=halves, tiled=True)]
    all_to_all x1, blocking collectives: 37.3 us -> 35.3 us  [per_device(): lax.all_to_all(result, 'fsdp', split_axis=0, concat_axis=0, tiled=True)]
    pallas_call x0 -> x1, Pallas kernels: none -> 1.64 us  [settle(): pl.pallas_call(copy_kernel, out_shape=jax.ShapeDtypeStruct(block.shape, b...]
    ppermute x3, waiting for transfers between devices: 14.8 us -> 13.7 us  [shifted(): return lax.ppermute(block, axis, route)]
    unnamed x4 -> x8, local copies, waits for them, and re-layouts: 1.92 us -> 2.62 us
  transfers between devices with their start and end apart: 7 -> 7, of which waited for: 4 -> 4; matrix products, arithmetic and copies ran while one was open for 5% -> 5% of each run, Pallas kernels for 0% -> 2%
where the time goes in v4:
time: 100 us; the launch traced here: 99.7 us
  blocking collectives  35.3 us (35%)
  waiting for transfers between devices  25.3 us (25%)
  starting transfers between devices  21.9 us (22%)
  matrix products  5.89 us (6%)
  local copies, waits for them, and re-layouts  5.4 us (5%)
  other arithmetic  4 us (4%)
  Pallas kernels  1.64 us (2%)
    all_to_all x1, blocking collectives, per_device(): lax.all_to_all(result, 'fsdp', split_axis=0, concat_axis=0, tiled=True)  35.3 us
    ppermute x3, waiting for transfers between devices, shifted(): return lax.ppermute(block, axis, route)  13.7 us
    all_to_all x2, starting transfers between devices, within(): lax.all_to_all(array, 'fsdp', 0, 0, axis_index_groups=halves, tiled=True)  11.7 us
    all_to_all x2, waiting for transfers between devices, within(): lax.all_to_all(array, 'fsdp', 0, 0, axis_index_groups=halves, tiled=True)  11.6 us
    ppermute x3, starting transfers between devices, shifted(): return lax.ppermute(block, axis, route)  3.73 us
    ppermute x1, starting transfers between devices, per_device(): far2 = settle(lax.ppermute(within(far2), 'fsdp', far), 20000000000)  3.29 us
    ppermute x1, starting transfers between devices, per_device(): far1 = lax.ppermute(far1, 'fsdp', far)  3.22 us
    dot_general x4, matrix products, orthogonalize(): jnp.dot(polynomial.astype(jnp.bfloat16), iterate, preferred_element_type=...  2.72 us
  transfers between devices with their start and end apart: 7, of which 4 were waited for; matrix products, arithmetic and copies ran while one was open for 5% of the time, Pallas kernels for 2%

profile of v4, /device:TPU:1, one launch (start us, length us, event | category | flops | bytes accessed | tf_op | source)
XLA Modules:
  0.0 99.7 jit_solution(6693651271854899831)
XLA Ops:
  0.0 0.9 copy.5
  0.9 1.1 %dynamic-slice_bitcast_fusion = bf16[8,8,5120]{2,1,0:T(8,128)(2,1)S(1)} fusion(bf16[1,16,8,5120]{3,2,1,0:T(8,128)(2,1)} %param.4, s32[]{:T(128)S(6)} %select_n.27), kind=kLoop, calls=%fused_computation.37 | loop fusion | bytes 1310724 | tf_op jit(solution)/shard_map/dynamic_slice | solution.py:88
  2.2 2.1 %collective-permute-start = (bf16[8,8,3328]{2,1,0:T(8,128)(2,1)S(1)}, bf16[8,8,3328]{2,1,0:T(8,128)(2,1)S(1)}, u32[]{:S(2)}, u32[]{:S(2)}) collective-permute-start(bf16[8,8,3328]{2,1,0:T(8,128)(2,1)S(1)} %multiply_convert_fusion.1), channel_id=1, source_target_pairs={{16,0},{0,16},{17,1},{1,17},{18,2},{2,18},{19,3},{3,19},{20,4},{4,... | collective-permute-start | bytes 1277960 | tf_op jit(solution)/shard_map/ppermute | solution.py:19
  4.6 0.2 multiply_convert_fusion
  4.8 1.5 %collective-permute-start.2 = (bf16[8,8,5120]{2,1,0:T(8,128)(2,1)S(1)}, bf16[8,8,5120]{2,1,0:T(8,128)(2,1)S(1)}, u32[]{:S(2)}, u32[]{:S(2)}) collective-permute-start(bf16[8,8,5120]{2,1,0:T(8,128)(2,1)S(1)} %multiply_convert_fusion), channel_id=1, source_target_pairs={{16,0},{0,16},{17,1},{1,17},{18,2},{2,18},{19,3},{3,19},{20,4},{4,... | collective-permute-start | bytes 1966088 | tf_op jit(solution)/shard_map/ppermute | solution.py:19
  6.3 1.4 %dynamic-slice_bitcast_fusion.1 = (bf16[8,8,5120]{2,1,0:T(8,128)(2,1)S(1)}, bf16[8,8,5120]{2,1,0:T(8,128)(2,1)S(1)}) fusion(bf16[1,16,8,5120]{3,2,1,0:T(8,128)(2,1)} %param.3, s32[]{:T(128)S(6)} %select_n.28, s32[]{:T(128)S(6)} %select_n.27), kind=kLoop, calls=%fused_computation.38 | loop fusion | bytes 2621448 | tf_op jit(solution)/shard_map/dynamic_slice | solution.py:88
  7.7 6.1 %collective-permute-done = bf16[8,8,3328]{2,1,0:T(8,128)(2,1)S(1)} collective-permute-done((bf16[8,8,3328]{2,1,0:T(8,128)(2,1)S(1)}, bf16[8,8,3328]{2,1,0:T(8,128)(2,1)S(1)}, u32[]{:S(2)}, u32[]{:S(2)}) %collective-permute-start) | collective-permute-done | bytes 426016 | tf_op jit(solution)/shard_map/ppermute | solution.py:19
  13.9 1.0 add_convert_fusion.1
  14.8 3.2 %collective-permute-start.3 = (bf16[8,8,3328]{2,1,0:T(8,128)(2,1)}, bf16[8,8,3328]{2,1,0:T(8,128)(2,1)S(1)}, u32[]{:S(2)}, u32[]{:S(2)}) collective-permute-start(bf16[8,8,3328]{2,1,0:T(8,128)(2,1)} %add_convert_fusion.1), channel_id=1, source_target_pairs={{0,12},{1,13},{2,14},{3,15},{4,8},{5,9},{6,10},{7,11},{8,4},{9,5},... | collective-permute-start | bytes 1277960 | tf_op jit(solution)/shard_map/ppermute | solution.py:110
  18.1 0.7 collective-permute-done.1
  18.8 0.8 add_convert_fusion.2
  19.6 6.4 %all-to-all-start.1 = ((bf16[8,8,1792]{2,1,0:T(8,128)(2,1)}), bf16[8,8,1792]{2,1,0:T(8,128)(2,1)S(1)}, u32[]{:S(2)}, u32[]{:S(2)}) async-start(bf16[8,8,1792]{2,1,0:T(8,128)(2,1)} %add_convert_fusion.2), calls=%async_computation.1 | async-start | bytes 458752 | tf_op jit(solution)/shard_map/all_to_all | solution.py:91
  26.0 6.8 %collective-permute-done.2 = bf16[8,8,5120]{2,1,0:T(8,128)(2,1)S(1)} collective-permute-done((bf16[8,8,5120]{2,1,0:T(8,128)(2,1)S(1)}, bf16[8,8,5120]{2,1,0:T(8,128)(2,1)S(1)}, u32[]{:S(2)}, u32[]{:S(2)}) %collective-permute-start.2) | collective-permute-done | bytes 655392 | tf_op jit(solution)/shard_map/ppermute | solution.py:19
  32.8 0.4 add_convert_fusion
  33.2 3.3 %collective-permute-start.4 = (bf16[8,8,1792]{2,1,0:T(8,128)(2,1)S(1)}, bf16[8,8,1792]{2,1,0:T(8,128)(2,1)S(1)}, u32[]{:S(2)}, u32[]{:S(2)}) collective-permute-start(bf16[8,8,1792]{2,1,0:T(8,128)(2,1)S(1)} %all-to-all-done.1), channel_id=1, source_target_pairs={{0,12},{1,13},{2,14},{3,15},{4,8},{5,9},{6,10},{7,11},{8,4},{9,5},... | collective-permute-start | bytes 688136 | tf_op jit(solution)/shard_map/ppermute | solution.py:111
  36.5 1.1 %pad_maximum_fusion = bf16[8,8,8448]{2,1,0:T(8,128)(2,1)} fusion(bf16[8,8,3328]{2,1,0:T(8,128)(2,1)S(1)} %collective-permute-done.3, bf16[8,8,5120]{2,1,0:T(8,128)(2,1)S(1)} %add_convert_fusion), kind=kLoop, calls=%fused_computation.34 | loop fusion | flops 2162688 | bytes 2162688 | tf_op jit(solution)/shard_map/concatenate | solution.py:114
  37.5 5.3 %all-to-all-start = ((bf16[8,8,8448]{2,1,0:T(8,128)(2,1)}), bf16[8,8,8448]{2,1,0:T(8,128)(2,1)S(1)}, u32[]{:S(2)}, u32[]{:S(2)}) async-start(bf16[8,8,8448]{2,1,0:T(8,128)(2,1)} %pad_maximum_fusion), calls=%async_computation | async-start | bytes 2162688 | tf_op jit(solution)/shard_map/all_to_all | solution.py:91
  42.8 0.7 copy-done.2
  43.5 1.6 %shard_map.37 = bf16[8,8,1792]{2,1,0:T(8,128)(2,1)} custom-call(bf16[8,8,1792]{2,1,0:T(8,128)(2,1)} %copy-done.2), custom_call_target="tpu_custom_call" | custom-call | flops 20000000000 | tf_op jit(solution)/shard_map/pallas_call | solution.py:36
  45.2 11.6 %all-to-all-done = bf16[8,8,8448]{2,1,0:T(8,128)(2,1)S(1)} async-done(((bf16[8,8,8448]{2,1,0:T(8,128)(2,1)}), bf16[8,8,8448]{2,1,0:T(8,128)(2,1)S(1)}, u32[]{:S(2)}, u32[]{:S(2)}) %all-to-all-start) | async-done | bytes 1081376 | tf_op jit(solution)/shard_map/all_to_all | solution.py:91
  57.0 0.5 fusion.50
  57.8 0.8 fusion.4
  58.6 0.5 convolution_convert_fusion.4
  59.2 0.6 fusion.1
  59.8 0.5 convolution_convert_fusion.3
  60.3 0.6 fusion.2
  60.9 0.5 convolution_convert_fusion.2
  61.5 0.6 fusion.3
  62.1 0.5 convolution_convert_fusion.1
  62.8 0.5 fusion.5
  63.3 35.3 %all_to_all.15 = bf16[16,8,5120]{2,1,0:T(8,128)(2,1)S(1)} all-to-all(bf16[16,8,5120]{2,1,0:T(8,128)(2,1)S(1)} %fusion.5), channel_id=1, replica_groups=mesh['rep'=2,'fsdp'=16] {'fsdp'}, dimensions={0} | all-to-all | bytes 2621440 | tf_op jit(solution)/shard_map/all_to_all | solution.py:125
  98.6 1.1 %copy.7 = bf16[1,16,8,5120]{3,2,1,0:T(8,128)(2,1)} copy(bf16[1,16,8,5120]{3,2,1,0:T(8,128)(2,1)S(1)} %bitcast.44) | data formatting | bytes 2621440
  (31 shorter events, 1.1 us)
Async XLA Ops:
  0.0 4.3 %copy-start = (bf16[1,16,8,5120]{3,2,1,0:T(8,128)(2,1)S(1)}, bf16[1,16,8,5120]{3,2,1,0:T(8,128)(2,1)}, u32[]{:S(2)}) copy-start(bf16[1,16,8,5120]{3,2,1,0:T(8,128)(2,1)} %param.4) | copy-start | bytes 3932164
  2.2 11.7 %collective-permute-start = (bf16[8,8,3328]{2,1,0:T(8,128)(2,1)S(1)}, bf16[8,8,3328]{2,1,0:T(8,128)(2,1)S(1)}, u32[]{:S(2)}, u32[]{:S(2)}) collective-permute-start(bf16[8,8,3328]{2,1,0:T(8,128)(2,1)S(1)} %multiply_convert_fusion.1), channel_id=1, source_target_pairs={{16,0},{0,16},{17,1},{1,17},{18,2},{2,18},{19,3},{3,19},{20,4},{4,... | collective-permute-start | bytes 1277960 | tf_op jit(solution)/shard_map/ppermute | solution.py:19
  4.5 14.3 %collective-permute-start.1 = (bf16[8,8,1792]{2,1,0:T(8,128)(2,1)S(1)}, bf16[8,8,1792]{2,1,0:T(8,128)(2,1)S(1)}, u32[]{:S(2)}, u32[]{:S(2)}) collective-permute-start(bf16[8,8,1792]{2,1,0:T(8,128)(2,1)S(1)} %multiply_convert_fusion.2), channel_id=1, source_target_pairs={{16,0},{0,16},{17,1},{1,17},{18,2},{2,18},{19,3},{3,19},{20,4},{4,... | collective-permute-start | bytes 688136 | tf_op jit(solution)/shard_map/ppermute | solution.py:19
  4.8 28.1 %collective-permute-start.2 = (bf16[8,8,5120]{2,1,0:T(8,128)(2,1)S(1)}, bf16[8,8,5120]{2,1,0:T(8,128)(2,1)S(1)}, u32[]{:S(2)}, u32[]{:S(2)}) collective-permute-start(bf16[8,8,5120]{2,1,0:T(8,128)(2,1)S(1)} %multiply_convert_fusion), channel_id=1, source_target_pairs={{16,0},{0,16},{17,1},{1,17},{18,2},{2,18},{19,3},{3,19},{20,4},{4,... | collective-permute-start | bytes 1966088 | tf_op jit(solution)/shard_map/ppermute | solution.py:19
  14.8 21.6 %collective-permute-start.3 = (bf16[8,8,3328]{2,1,0:T(8,128)(2,1)}, bf16[8,8,3328]{2,1,0:T(8,128)(2,1)S(1)}, u32[]{:S(2)}, u32[]{:S(2)}) collective-permute-start(bf16[8,8,3328]{2,1,0:T(8,128)(2,1)} %add_convert_fusion.1), channel_id=1, source_target_pairs={{0,12},{1,13},{2,14},{3,15},{4,8},{5,9},{6,10},{7,11},{8,4},{9,5},... | collective-permute-start | bytes 1277960 | tf_op jit(solution)/shard_map/ppermute | solution.py:110
  19.6 13.6 %all-to-all-start.1 = ((bf16[8,8,1792]{2,1,0:T(8,128)(2,1)}), bf16[8,8,1792]{2,1,0:T(8,128)(2,1)S(1)}, u32[]{:S(2)}, u32[]{:S(2)}) async-start(bf16[8,8,1792]{2,1,0:T(8,128)(2,1)} %add_convert_fusion.2), calls=%async_computation.1 | async-start | bytes 458752 | tf_op jit(solution)/shard_map/all_to_all | solution.py:91
  33.2 9.6 %collective-permute-start.4 = (bf16[8,8,1792]{2,1,0:T(8,128)(2,1)S(1)}, bf16[8,8,1792]{2,1,0:T(8,128)(2,1)S(1)}, u32[]{:S(2)}, u32[]{:S(2)}) collective-permute-start(bf16[8,8,1792]{2,1,0:T(8,128)(2,1)S(1)} %all-to-all-done.1), channel_id=1, source_target_pairs={{0,12},{1,13},{2,14},{3,15},{4,8},{5,9},{6,10},{7,11},{8,4},{9,5},... | collective-permute-start | bytes 688136 | tf_op jit(solution)/shard_map/ppermute | solution.py:111
  37.5 19.3 %all-to-all-start = ((bf16[8,8,8448]{2,1,0:T(8,128)(2,1)}), bf16[8,8,8448]{2,1,0:T(8,128)(2,1)S(1)}, u32[]{:S(2)}, u32[]{:S(2)}) async-start(bf16[8,8,8448]{2,1,0:T(8,128)(2,1)} %pad_maximum_fusion), calls=%async_computation | async-start | bytes 2162688 | tf_op jit(solution)/shard_map/all_to_all | solution.py:91
  42.8 0.7 copy-start.2
  45.2 11.7 %copy-start.1 = (bf16[8,8,1792]{2,1,0:T(8,128)(2,1)S(1)}, bf16[8,8,1792]{2,1,0:T(8,128)(2,1)}, u32[]{:S(2)}) copy-start(bf16[8,8,1792]{2,1,0:T(8,128)(2,1)} %shard_map.37) | copy-start | bytes 688132

commit v5 on v4

--- a/solution.py
+++ b/solution.py
@@ -43,28 +43,42 @@
 
 
 def orthogonalize(matrix, order, rows, columns):
-    f32 = jnp.float32
+    f32, bf16 = jnp.float32, jnp.bfloat16
     factor = 2.0 ** (int(math.log2(columns)) // 2)
     eye = jnp.eye(matrix.shape[0], dtype=f32)
-    iterate = matrix
-    for iteration in range(NS_STEPS):
-        last = iteration == NS_STEPS - 1
-        gram = lax.dot_general(iterate, iterate, (((1,), (1,)), ((), ())), preferred_element_type=f32)
-        scale = 1.0
-        if iteration == 0:
-            gram = lax.optimization_barrier(gram)
-            trace = jnp.broadcast_to(jnp.sum(gram * eye, axis=0, keepdims=True), (rows, gram.shape[1]))
-            trace = jnp.sum(lax.optimization_barrier(trace), axis=1, keepdims=True)
-            scale = jnp.tile(1.0 / (jnp.sqrt(trace) + 1e-07), (gram.shape[0] // rows, 1))
-            gram = gram * (scale * scale)
-        gram = gram.astype(jnp.bfloat16)
-        square = jnp.dot(gram, gram, preferred_element_type=f32)
-        polynomial = coef_b * gram.astype(f32) + coef_c * square
-        if last:
-            polynomial = order((coef_a * eye + polynomial) * factor).astype(jnp.bfloat16)
-            return jnp.dot(polynomial, iterate, preferred_element_type=f32).astype(jnp.bfloat16)
-        product = jnp.dot(polynomial.astype(jnp.bfloat16), iterate, preferred_element_type=f32)
-        iterate = ((coef_a * iterate.astype(f32) + product) * scale).astype(jnp.bfloat16)
+
+    def dot(left, right):
+        return jnp.dot(left.astype(bf16), right.astype(bf16), preferred_element_type=f32)
+
+    def fine(left, right):
+        return jnp.dot(left, right, precision=lax.Precision.HIGH, preferred_element_type=f32)
+
+    def polynomial_of(gram):
+        return coef_b * gram + coef_c * dot(gram, gram)
+
+    def gram_of(block):
+        return lax.dot_general(block, block, (((1,), (1,)), ((), ())), preferred_element_type=f32)
+
+    gram = lax.optimization_barrier(gram_of(matrix))
+    trace = jnp.broadcast_to(jnp.sum(gram * eye, axis=0, keepdims=True), (rows, gram.shape[1]))
+    trace = jnp.sum(lax.optimization_barrier(trace), axis=1, keepdims=True)
+    scale = jnp.tile(1.0 / (jnp.sqrt(trace) + 1e-07), (gram.shape[0] // rows, 1))
+    gram = (gram * (scale * scale)).astype(bf16).astype(f32)
+    first = polynomial_of(gram)
+    step = coef_a * eye + first
+    second = polynomial_of(fine(step, fine(gram, step)))
+    both = coef_a * (first + second) + fine(second, first)
+    product = jnp.dot((both * scale).astype(bf16), matrix, preferred_element_type=f32)
+    iterate = ((coef_a * coef_a * scale) * matrix.astype(f32) + product).astype(bf16)
+    for iteration in range(2, NS_STEPS):
+        gram = gram_of(iterate).astype(bf16).astype(f32)
+        polynomial = polynomial_of(gram)
+        if iteration == NS_STEPS - 1:
+            polynomial = order((coef_a * eye + polynomial) * factor).astype(bf16)
+            polynomial = lax.optimization_barrier(polynomial)
+            return jnp.dot(polynomial, iterate, preferred_element_type=f32).astype(bf16)
+        product = jnp.dot(polynomial.astype(bf16), iterate, preferred_element_type=f32)
+        iterate = (coef_a * iterate.astype(f32) + product).astype(bf16)
 
 
 def per_device(tracker, levels, exponents):

time: 100 us -> 99.6 us (level)
    dot_general x11 -> x14, matrix products: 5.89 us -> 5.36 us  [the longest x4 2.02 us: gram_of(): lax.dot_general(block, block, (((1,), (1,)), ((), ())), preferred_element...]
where the time goes in v5:
time: 99.6 us; the launch traced here: 99.2 us
  blocking collectives  35.4 us (36%)
  waiting for transfers between devices  25.3 us (25%)
  starting transfers between devices  21.9 us (22%)
  local copies, waits for them, and re-layouts  5.39 us (5%)
  matrix products  5.36 us (5%)
  other arithmetic  4 us (4%)
  Pallas kernels  1.65 us (2%)
    all_to_all x1, blocking collectives, per_device(): lax.all_to_all(result, 'fsdp', split_axis=0, concat_axis=0, tiled=True)  35.4 us
    ppermute x3, waiting for transfers between devices, shifted(): return lax.ppermute(block, axis, route)  13.7 us
    all_to_all x2, starting transfers between devices, within(): lax.all_to_all(array, 'fsdp', 0, 0, axis_index_groups=halves, tiled=True)  11.7 us
    all_to_all x2, waiting for transfers between devices, within(): lax.all_to_all(array, 'fsdp', 0, 0, axis_index_groups=halves, tiled=True)  11.6 us
    ppermute x3, starting transfers between devices, shifted(): return lax.ppermute(block, axis, route)  3.73 us
    ppermute x1, starting transfers between devices, per_device(): far2 = settle(lax.ppermute(within(far2), 'fsdp', far), 20000000000)  3.29 us
    ppermute x1, starting transfers between devices, per_device(): far1 = lax.ppermute(far1, 'fsdp', far)  3.22 us
    unnamed x8, local copies, waits for them, and re-layouts  2.61 us
  transfers between devices with their start and end apart: 7, of which 4 were waited for; matrix products, arithmetic and copies ran while one was open for 5% of the time, Pallas kernels for 2%

profile of v5, /device:TPU:1, one launch (start us, length us, event | category | flops | bytes accessed | tf_op | source)
XLA Modules:
  0.0 99.2 jit_solution(17100092973836356587)
XLA Ops:
  0.0 0.9 copy.5
  0.9 1.1 %dynamic-slice_bitcast_fusion = bf16[8,8,5120]{2,1,0:T(8,128)(2,1)S(1)} fusion(bf16[1,16,8,5120]{3,2,1,0:T(8,128)(2,1)} %param.4, s32[]{:T(128)S(6)} %select_n.27), kind=kLoop, calls=%fused_computation.34 | loop fusion | bytes 1310724 | tf_op jit(solution)/shard_map/dynamic_slice | solution.py:102
  2.2 2.1 %collective-permute-start = (bf16[8,8,3328]{2,1,0:T(8,128)(2,1)S(1)}, bf16[8,8,3328]{2,1,0:T(8,128)(2,1)S(1)}, u32[]{:S(2)}, u32[]{:S(2)}) collective-permute-start(bf16[8,8,3328]{2,1,0:T(8,128)(2,1)S(1)} %multiply_convert_fusion.1), channel_id=1, source_target_pairs={{16,0},{0,16},{17,1},{1,17},{18,2},{2,18},{19,3},{3,19},{20,4},{4,... | collective-permute-start | bytes 1277960 | tf_op jit(solution)/shard_map/ppermute | solution.py:19
  4.8 1.5 %collective-permute-start.2 = (bf16[8,8,5120]{2,1,0:T(8,128)(2,1)S(1)}, bf16[8,8,5120]{2,1,0:T(8,128)(2,1)S(1)}, u32[]{:S(2)}, u32[]{:S(2)}) collective-permute-start(bf16[8,8,5120]{2,1,0:T(8,128)(2,1)S(1)} %multiply_convert_fusion), channel_id=1, source_target_pairs={{16,0},{0,16},{17,1},{1,17},{18,2},{2,18},{19,3},{3,19},{20,4},{4,... | collective-permute-start | bytes 1966088 | tf_op jit(solution)/shard_map/ppermute | solution.py:19
  6.3 1.4 %dynamic-slice_bitcast_fusion.1 = (bf16[8,8,5120]{2,1,0:T(8,128)(2,1)S(1)}, bf16[8,8,5120]{2,1,0:T(8,128)(2,1)S(1)}) fusion(bf16[1,16,8,5120]{3,2,1,0:T(8,128)(2,1)} %param.3, s32[]{:T(128)S(6)} %select_n.28, s32[]{:T(128)S(6)} %select_n.27), kind=kLoop, calls=%fused_computation.35 | loop fusion | bytes 2621448 | tf_op jit(solution)/shard_map/dynamic_slice | solution.py:102
  7.7 6.1 %collective-permute-done = bf16[8,8,3328]{2,1,0:T(8,128)(2,1)S(1)} collective-permute-done((bf16[8,8,3328]{2,1,0:T(8,128)(2,1)S(1)}, bf16[8,8,3328]{2,1,0:T(8,128)(2,1)S(1)}, u32[]{:S(2)}, u32[]{:S(2)}) %collective-permute-start) | collective-permute-done | bytes 426016 | tf_op jit(solution)/shard_map/ppermute | solution.py:19
  13.9 1.0 %add_convert_fusion.1 = bf16[8,8,3328]{2,1,0:T(8,128)(2,1)} fusion(bf16[8,8,3328]{2,1,0:T(8,128)(2,1)S(1)} %multiply_convert_fusion.1, bf16[8,8,3328]{2,1,0:T(8,128)(2,1)S(1)} %collective-permute-done, bf16[8,8,3328]{2,1,0:T(8,128)(2,1)S(1)} %slice.73), kind=kLoop, calls=%fused_computation.32 | loop fusion | flops 1916928 | bytes 1703936 | tf_op jit(solution)/shard_map/convert_element_type | solution.py:27
  14.8 3.2 %collective-permute-start.3 = (bf16[8,8,3328]{2,1,0:T(8,128)(2,1)}, bf16[8,8,3328]{2,1,0:T(8,128)(2,1)S(1)}, u32[]{:S(2)}, u32[]{:S(2)}) collective-permute-start(bf16[8,8,3328]{2,1,0:T(8,128)(2,1)} %add_convert_fusion.1), channel_id=1, source_target_pairs={{0,12},{1,13},{2,14},{3,15},{4,8},{5,9},{6,10},{7,11},{8,4},{9,5},... | collective-permute-start | bytes 1277960 | tf_op jit(solution)/shard_map/ppermute | solution.py:124
  18.1 0.7 collective-permute-done.1
  18.8 0.8 add_convert_fusion.2
  19.6 6.4 %all-to-all-start.1 = ((bf16[8,8,1792]{2,1,0:T(8,128)(2,1)}), bf16[8,8,1792]{2,1,0:T(8,128)(2,1)S(1)}, u32[]{:S(2)}, u32[]{:S(2)}) async-start(bf16[8,8,1792]{2,1,0:T(8,128)(2,1)} %add_convert_fusion.2), calls=%async_computation.1 | async-start | bytes 458752 | tf_op jit(solution)/shard_map/all_to_all | solution.py:105
  26.0 6.9 %collective-permute-done.2 = bf16[8,8,5120]{2,1,0:T(8,128)(2,1)S(1)} collective-permute-done((bf16[8,8,5120]{2,1,0:T(8,128)(2,1)S(1)}, bf16[8,8,5120]{2,1,0:T(8,128)(2,1)S(1)}, u32[]{:S(2)}, u32[]{:S(2)}) %collective-permute-start.2) | collective-permute-done | bytes 655392 | tf_op jit(solution)/shard_map/ppermute | solution.py:19
  32.8 0.4 add_convert_fusion
  33.2 3.3 %collective-permute-start.4 = (bf16[8,8,1792]{2,1,0:T(8,128)(2,1)S(1)}, bf16[8,8,1792]{2,1,0:T(8,128)(2,1)S(1)}, u32[]{:S(2)}, u32[]{:S(2)}) collective-permute-start(bf16[8,8,1792]{2,1,0:T(8,128)(2,1)S(1)} %all-to-all-done.1), channel_id=1, source_target_pairs={{0,12},{1,13},{2,14},{3,15},{4,8},{5,9},{6,10},{7,11},{8,4},{9,5},... | collective-permute-start | bytes 688136 | tf_op jit(solution)/shard_map/ppermute | solution.py:125
  36.5 1.1 %pad_maximum_fusion = bf16[8,8,8448]{2,1,0:T(8,128)(2,1)} fusion(bf16[8,8,3328]{2,1,0:T(8,128)(2,1)S(1)} %collective-permute-done.3, bf16[8,8,5120]{2,1,0:T(8,128)(2,1)S(1)} %add_convert_fusion), kind=kLoop, calls=%fused_computation.31 | loop fusion | flops 2162688 | bytes 2162688 | tf_op jit(solution)/shard_map/concatenate | solution.py:128
  37.5 5.3 %all-to-all-start = ((bf16[8,8,8448]{2,1,0:T(8,128)(2,1)}), bf16[8,8,8448]{2,1,0:T(8,128)(2,1)S(1)}, u32[]{:S(2)}, u32[]{:S(2)}) async-start(bf16[8,8,8448]{2,1,0:T(8,128)(2,1)} %pad_maximum_fusion), calls=%async_computation | async-start | bytes 2162688 | tf_op jit(solution)/shard_map/all_to_all | solution.py:105
  42.8 0.7 copy-done.2
  43.5 1.6 %shard_map.37 = bf16[8,8,1792]{2,1,0:T(8,128)(2,1)} custom-call(bf16[8,8,1792]{2,1,0:T(8,128)(2,1)} %copy-done.2), custom_call_target="tpu_custom_call" | custom-call | flops 20000000000 | tf_op jit(solution)/shard_map/pallas_call | solution.py:36
  45.2 11.6 %all-to-all-done = bf16[8,8,8448]{2,1,0:T(8,128)(2,1)S(1)} async-done(((bf16[8,8,8448]{2,1,0:T(8,128)(2,1)}), bf16[8,8,8448]{2,1,0:T(8,128)(2,1)S(1)}, u32[]{:S(2)}, u32[]{:S(2)}) %all-to-all-start) | async-done | bytes 1081376 | tf_op jit(solution)/shard_map/all_to_all | solution.py:105
  57.0 0.5 fusion.42
  57.8 0.2 fusion.11
  58.0 0.2 fusion.21
  58.6 0.2 fusion.12
  58.8 0.5 fusion
  59.3 0.5 convolution_convert_fusion.3
  59.8 0.6 fusion.1
  60.4 0.5 convolution_convert_fusion.2
  60.9 0.6 fusion.2
  61.6 0.5 convolution_convert_fusion.1
  62.3 0.5 fusion.3
  62.8 35.4 %all_to_all.15 = bf16[16,8,5120]{2,1,0:T(8,128)(2,1)S(1)} all-to-all(bf16[16,8,5120]{2,1,0:T(8,128)(2,1)S(1)} %fusion.3), channel_id=1, replica_groups=mesh['rep'=2,'fsdp'=16] {'fsdp'}, dimensions={0} | all-to-all | bytes 2621440 | tf_op jit(solution)/shard_map/all_to_all | solution.py:139
  98.1 1.1 %copy.7 = bf16[1,16,8,5120]{3,2,1,0:T(8,128)(2,1)} copy(bf16[1,16,8,5120]{3,2,1,0:T(8,128)(2,1)S(1)} %bitcast.44) | data formatting | bytes 2621440
  (35 shorter events, 1.6 us)
Async XLA Ops:
  0.0 4.3 %copy-start = (bf16[1,16,8,5120]{3,2,1,0:T(8,128)(2,1)S(1)}, bf16[1,16,8,5120]{3,2,1,0:T(8,128)(2,1)}, u32[]{:S(2)}) copy-start(bf16[1,16,8,5120]{3,2,1,0:T(8,128)(2,1)} %param.4) | copy-start | bytes 3932164
  2.2 11.7 %collective-permute-start = (bf16[8,8,3328]{2,1,0:T(8,128)(2,1)S(1)}, bf16[8,8,3328]{2,1,0:T(8,128)(2,1)S(1)}, u32[]{:S(2)}, u32[]{:S(2)}) collective-permute-start(bf16[8,8,3328]{2,1,0:T(8,128)(2,1)S(1)} %multiply_convert_fusion.1), channel_id=1, source_target_pairs={{16,0},{0,16},{17,1},{1,17},{18,2},{2,18},{19,3},{3,19},{20,4},{4,... | collective-permute-start | bytes 1277960 | tf_op jit(solution)/shard_map/ppermute | solution.py:19
  4.5 14.3 %collective-permute-start.1 = (bf16[8,8,1792]{2,1,0:T(8,128)(2,1)S(1)}, bf16[8,8,1792]{2,1,0:T(8,128)(2,1)S(1)}, u32[]{:S(2)}, u32[]{:S(2)}) collective-permute-start(bf16[8,8,1792]{2,1,0:T(8,128)(2,1)S(1)} %multiply_convert_fusion.2), channel_id=1, source_target_pairs={{16,0},{0,16},{17,1},{1,17},{18,2},{2,18},{19,3},{3,19},{20,4},{4,... | collective-permute-start | bytes 688136 | tf_op jit(solution)/shard_map/ppermute | solution.py:19
  4.8 28.1 %collective-permute-start.2 = (bf16[8,8,5120]{2,1,0:T(8,128)(2,1)S(1)}, bf16[8,8,5120]{2,1,0:T(8,128)(2,1)S(1)}, u32[]{:S(2)}, u32[]{:S(2)}) collective-permute-start(bf16[8,8,5120]{2,1,0:T(8,128)(2,1)S(1)} %multiply_convert_fusion), channel_id=1, source_target_pairs={{16,0},{0,16},{17,1},{1,17},{18,2},{2,18},{19,3},{3,19},{20,4},{4,... | collective-permute-start | bytes 1966088 | tf_op jit(solution)/shard_map/ppermute | solution.py:19
  14.8 21.6 %collective-permute-start.3 = (bf16[8,8,3328]{2,1,0:T(8,128)(2,1)}, bf16[8,8,3328]{2,1,0:T(8,128)(2,1)S(1)}, u32[]{:S(2)}, u32[]{:S(2)}) collective-permute-start(bf16[8,8,3328]{2,1,0:T(8,128)(2,1)} %add_convert_fusion.1), channel_id=1, source_target_pairs={{0,12},{1,13},{2,14},{3,15},{4,8},{5,9},{6,10},{7,11},{8,4},{9,5},... | collective-permute-start | bytes 1277960 | tf_op jit(solution)/shard_map/ppermute | solution.py:124
  19.6 13.6 %all-to-all-start.1 = ((bf16[8,8,1792]{2,1,0:T(8,128)(2,1)}), bf16[8,8,1792]{2,1,0:T(8,128)(2,1)S(1)}, u32[]{:S(2)}, u32[]{:S(2)}) async-start(bf16[8,8,1792]{2,1,0:T(8,128)(2,1)} %add_convert_fusion.2), calls=%async_computation.1 | async-start | bytes 458752 | tf_op jit(solution)/shard_map/all_to_all | solution.py:105
  33.2 9.6 %collective-permute-start.4 = (bf16[8,8,1792]{2,1,0:T(8,128)(2,1)S(1)}, bf16[8,8,1792]{2,1,0:T(8,128)(2,1)S(1)}, u32[]{:S(2)}, u32[]{:S(2)}) collective-permute-start(bf16[8,8,1792]{2,1,0:T(8,128)(2,1)S(1)} %all-to-all-done.1), channel_id=1, source_target_pairs={{0,12},{1,13},{2,14},{3,15},{4,8},{5,9},{6,10},{7,11},{8,4},{9,5},... | collective-permute-start | bytes 688136 | tf_op jit(solution)/shard_map/ppermute | solution.py:125
  37.5 19.3 %all-to-all-start = ((bf16[8,8,8448]{2,1,0:T(8,128)(2,1)}), bf16[8,8,8448]{2,1,0:T(8,128)(2,1)S(1)}, u32[]{:S(2)}, u32[]{:S(2)}) async-start(bf16[8,8,8448]{2,1,0:T(8,128)(2,1)} %pad_maximum_fusion), calls=%async_computation | async-start | bytes 2162688 | tf_op jit(solution)/shard_map/all_to_all | solution.py:105
  42.8 0.7 copy-start.2
  45.2 11.7 %copy-start.1 = (bf16[8,8,1792]{2,1,0:T(8,128)(2,1)S(1)}, bf16[8,8,1792]{2,1,0:T(8,128)(2,1)}, u32[]{:S(2)}) copy-start(bf16[8,8,1792]{2,1,0:T(8,128)(2,1)} %shard_map.37) | copy-start | bytes 688132
